TPU v7x, 32 devices: a whole 2x2x4 slice. The times are simulated.
32 devices in a mesh: freq: 4 (over y, x), blk: 8 (over z, core).
Axes of the slice: x: 2, y: 2, z: 4, core: 2. Of those that a mesh axis runs over, the one named last changes fastest.
Arguments:
- voltages: float32 [32, 32, 2, 128, 256], P('blk', None, None, 'freq'), may hold values from -6 to 6
- pair_table: int32 [528, 2], P('blk'), may hold values from 0 to 31, as said below
- bad_feeds: int32 [64], replicated, may hold values from 0 to 2047
Outputs:
- visibilities: float32 [528, 32, 2, 128, 128], P('blk', 'freq')
Inputs may be any that keep to these rules, and one draw needn't show every extreme that they name: `pair_table`: device k of blk holds blocks k * 4 to k * 4 + 3 and tiles k * 66 to k * 66 + 65. Of its tiles, the first 4 (5) / 2 name two of its own blocks; then for d = 1 to 3 in turn, 16 tiles each name one own block and one block of device k + d; the last (17) / 2 name one own block and one block of device k + 4; device numbers are taken modulo 32 / 4, and either block of a tile may come first. Every unordered pair of blocks is named at least once.
All inputs are finite; a program needn't handle non-finite values.
Results may differ from a plain program's by a relative error of at most 0.000098.
Values sent between devices are 32-bit elements; how exact they have to be, the bound alone decides.
A program may use at most 320 MiB of HBM per device.

v0:
```python
import jax
import jax.numpy as jnp
from jax import lax
from jax.sharding import PartitionSpec as P


def passed_along(value, axis, steps):
    count = lax.axis_size(axis)
    pairs = [(source, (source + steps) % count) for source in range(count)]
    return lax.ppermute(value, axis, pairs)


def correlate(left, right):
    scale = 1.0 / left.shape[-1]
    prec = lax.Precision.HIGHEST
    left_re = left[:, :, 0]
    left_im = left[:, :, 1]
    stacked = jnp.stack([jnp.stack([left_re, left_im], 2), jnp.stack([left_im, -left_re], 2)], 2)
    return jnp.einsum("gcokps,gckqs->gcopq", stacked, right, precision=prec) * scale


def shards(voltages, pair_table, bad_feeds):
    blk_count = lax.axis_size("blk")
    moved = lax.all_to_all(voltages, "freq", split_axis=1, concat_axis=3, tiled=True)
    per_dev, chan_dev, _, width, samples = moved.shape
    here = lax.axis_index("blk")
    inputs = (here * per_dev + jnp.arange(per_dev, dtype=jnp.int32))[:, None] * width + jnp.arange(
        width, dtype=jnp.int32
    )[None, :]
    flagged = jnp.any((inputs // 2)[:, :, None] == bad_feeds[None, None, :], axis=-1)
    keep = jnp.where(flagged, 0.0, 1.0).astype(jnp.float32)
    own_blocks = moved * keep[:, None, None, :, None]
    tile_count = per_dev * per_dev
    own_count = per_dev * (per_dev + 1) // 2
    shared_count = (tile_count + 1) // 2
    half = blk_count // 2
    sign = jnp.array([1.0, -1.0], jnp.float32)[:, None, None]

    def correlate_group(pair_rows, far_blocks):
        swapped = pair_rows[:, 0] // per_dev != here
        own_local = jnp.where(swapped, pair_rows[:, 1], pair_rows[:, 0]) % per_dev
        far_local = jnp.where(swapped, pair_rows[:, 0], pair_rows[:, 1]) % per_dev
        tile = correlate(
            jnp.take(own_blocks, own_local, axis=0), jnp.take(far_blocks, far_local, axis=0)
        )
        flipped = jnp.swapaxes(tile, -1, -2) * sign
        return jnp.where(swapped[:, None, None, None, None], flipped, tile)

    def place_group(visibility, start, count, far_blocks):
        pair_rows = lax.dynamic_slice_in_dim(pair_table, start, count, 0)
        return lax.dynamic_update_slice_in_dim(
            visibility, correlate_group(pair_rows, far_blocks), start, 0
        )

    visibility = jnp.zeros((pair_table.shape[0], chan_dev, 2, width, width), jnp.float32)
    visibility = place_group(visibility, 0, own_count, own_blocks)

    def advance(buffer):
        return passed_along(buffer, "blk", -1)

    def forward_chain(step, carry):
        buffer, visibility = carry
        buffer = advance(buffer)
        return (
            buffer,
            place_group(visibility, own_count + (step - 1) * tile_count, tile_count, buffer),
        )

    buffer, visibility = lax.fori_loop(1, half, forward_chain, (own_blocks, visibility))
    buffer = advance(buffer)
    visibility = place_group(visibility, own_count + (half - 1) * tile_count, shared_count, buffer)
    return visibility


def solution(mesh):
    placed = (P("blk", None, None, "freq", None), P("blk", None), P())
    return jax.shard_map(
        shards,
        mesh=mesh,
        in_specs=placed,
        out_specs=P("blk", "freq", None, None, None),
        check_vma=False,
    )
```

profile of v0, /device:TPU:0, one launch (start us, length us, event | category | flops | bytes accessed | tf_op | source)
XLA Modules:
  0.0 1167.7 jit_solution(14731499237473493963)
XLA Ops:
  0.0 8.5 copy.22
  8.5 5.7 all-to-all-start
  14.4 93.6 %all-to-all-done = f32[4,32,2,32,256]{4,3,2,0,1:T(8,128)} async-done(((f32[4,32,2,32,256]{4,3,2,0,1:T(8,128)}), f32[4,32,2,32,256]{4,3,2,0,1:T(8,128)}, u32[]{:S(2)}, u32[]{:S(2)}) %all-to-all-start) | async-done | bytes 8388640 | tf_op jit(solution)/shard_map/all_to_all | solution.py:24
  108.0 4.3 copy.23
  112.3 5.2 bitcast_multiply_fusion
  117.5 12.8 %gather_fusion.2 = f32[10,8,2,128,256]{4,3,2,1,0:T(8,128)} fusion(f32[4,8,2,128,256]{4,3,2,1,0:T(8,128)} %bitcast_multiply_fusion, s32[1024]{0:T(1024)S(1)} %pad_clamp_fusion.5), kind=kCustom, calls=%fused_computation.clone | custom fusion | bytes 41943080 | tf_op jit(solution)/shard_map/jit(_take)/gather | solution.py:44
  130.3 16.4 %broadcast_select_fusion.1 = f32[10,8,2,128,256]{4,3,2,1,0:T(8,128)} fusion(f32[10,8,2,128,256]{4,3,2,1,0:T(8,128)} %gather_fusion.2, pred[10]{0:T(512)(128)(4,1)S(1)} %get-tuple-element.314), kind=kLoop, calls=%fused_computation.62 | loop fusion | flops 5242880 | bytes 41943048 | tf_op jit(solution)/shard_map/jit(_take)/select_n | solution.py:44
  146.7 16.8 %fusion.67 = f32[10,8,1,2,128,256]{5,4,3,2,1,0:T(8,128)} fusion(f32[10,8,2,128,256]{4,3,2,1,0:T(8,128)} %gather_fusion.2, pred[10]{0:T(512)(128)(4,1)S(1)} %get-tuple-element.314), kind=kLoop, calls=%fused_computation.138 | loop fusion | flops 5242880 | bytes 41943048 | tf_op jit(solution)/shard_map/stack | solution.py:18
  163.5 3.3 copy.38
  166.8 13.8 %fusion.63 = (f32[10,8,1,128,256]{4,3,2,1,0:T(8,128)}, f32[10,8,1,128,256]{4,3,2,1,0:T(8,128)}) fusion(f32[10,8,2,128,256]{4,3,2,1,0:T(8,128)} %broadcast_select_fusion.1), kind=kLoop, calls=%fused_computation.134 | loop fusion | flops 2621440 | bytes 41943040 | tf_op jit(solution)/shard_map/slice | solution.py:17
  180.6 12.9 %gather_fusion.3 = f32[10,8,2,128,256]{4,3,2,1,0:T(8,128)} fusion(f32[4,8,2,128,256]{4,3,2,1,0:T(8,128)} %bitcast_multiply_fusion, s32[1024]{0:T(1024)S(1)} %pad_clamp_fusion.4), kind=kCustom, calls=%fused_computation.3.clone | custom fusion | bytes 41943080 | tf_op jit(solution)/shard_map/jit(_take)/gather | solution.py:44
  193.6 16.1 %maximum_bitcast_fusion.1 = f32[10,8,1,2,128,256]{5,4,3,2,1,0:T(8,128)} fusion(f32[10,8,1,128,256]{4,3,2,1,0:T(8,128)} %get-tuple-element.322, f32[10,8,1,128,256]{4,3,2,1,0:T(8,128)} %get-tuple-element.321), kind=kLoop, calls=%fused_computation.53 | loop fusion | flops 5242880 | bytes 41943040 | tf_op jit(solution)/shard_map/stack | solution.py:18
  209.6 44.6 %fusion.36 = f32[10,8,2,128,128]{4,3,2,1,0:T(8,128)} fusion(f32[10,8,2,128,256]{4,3,2,1,0:T(8,128)} %gather_fusion.3, pred[10]{0:T(512)(128)(4,1)S(1)} %get-tuple-element.317, f32[10,8,1,2,128,256]{5,4,3,2,1,0:T(8,128)} %maximum_bitcast_fusion.1, f32[10,8,1,2,128,256]{5,4,3,2,1,0:T(8,128)} %fusion.67), kind=kOutput, calls=%fused_computation.71 | convolution fusion | flops 16121856000 | bytes 73400328 | tf_op jit(solution)/shard_map/gcokps,gckqs->gcopq/dot_general | solution.py:19
  254.3 11.3 copy.25
  265.5 8.2 bitcast_select_fusion.3
  273.8 22.3 %dynamic_update_slice.20 = f32[66,8,2,128,128]{4,3,2,1,0:T(8,128)} pad(f32[10,8,2,128,128]{4,3,2,1,0:T(8,128)S(1)} %bitcast_select_fusion.3, f32[]{:T(128)} %constant.272.clone.1), padding=0_56x0_0x0_0x0_0x0_0 | pad | bytes 79691776 | tf_op jit(solution)/shard_map/dynamic_update_slice | solution.py:51
  296.1 709.5 %while.21 = (s32[]{:T(128)}, f32[4,8,2,128,256]{4,3,2,1,0:T(8,128)}, f32[66,8,2,128,128]{4,3,2,1,0:T(8,128)}, s32[66,2]{0,1:T(2,128)S(1)}, s32[]{:T(128)}, /*ind...) while((s32[]{:T(128)}, ...), condition=%wide.region_2.5_spmd.clone, body=%wide.region_1.4_spmd.sunk.clone.sunk | while | flops 25836914688 | bytes 754986880 | solution.py:69
  296.1 2.6 collective-permute-start
  299.4 16.4 %gather_fusion.1 = f32[16,8,2,128,256]{4,3,2,1,0:T(8,128)} fusion(f32[4,8,2,128,256]{4,3,2,1,0:T(8,128)} %get-tuple-element.405, s32[1024]{0:T(1024)S(1)} %pad_clamp_fusion.9), kind=kCustom, calls=%fused_computation.1.clone.clone.1 | custom fusion | bytes 67108928 | tf_op jit(solution)/shard_map/while/body/eval_jaxpr/jit(_take)/gather | solution.py:44
  315.8 23.4 %broadcast_select_fusion.5 = f32[16,8,2,128,256]{4,3,2,1,0:T(8,128)} fusion(f32[16,8,2,128,256]{4,3,2,1,0:T(8,128)} %gather_fusion.1, pred[16]{0:T(512)(128)(4,1)S(1)} %get-tuple-element.373), kind=kLoop, calls=%fused_computation.17.clone.2 | loop fusion | flops 8388608 | bytes 67108880 | tf_op jit(solution)/shard_map/while/body/eval_jaxpr/jit(_take)/select_n | solution.py:44
  339.2 21.4 %fusion.82 = (f32[16,8,1,128,256]{4,3,2,1,0:T(8,128)}, f32[16,8,1,128,256]{4,3,2,1,0:T(8,128)}) fusion(f32[16,8,2,128,256]{4,3,2,1,0:T(8,128)} %broadcast_select_fusion.5), kind=kLoop, calls=%fused_computation.133.clone.1 | loop fusion | flops 4194304 | bytes 67108864 | tf_op jit(solution)/shard_map/while/body/eval_jaxpr/slice | solution.py:17
  360.7 26.8 %maximum_bitcast_fusion.4 = f32[16,8,1,2,128,256]{5,4,3,2,1,0:T(8,128)} fusion(f32[16,8,1,128,256]{4,3,2,1,0:T(8,128)} %get-tuple-element.374, f32[16,8,1,128,256]{4,3,2,1,0:T(8,128)} %get-tuple-element.375), kind=kLoop, calls=%fused_computation.10.clone.1 | loop fusion | flops 8388608 | bytes 67108864 | tf_op jit(solution)/shard_map/while/body/eval_jaxpr/stack | solution.py:18
  387.5 1.5 slice-done.4
  392.6 11.3 fusion.83
  403.9 16.2 %gather_fusion = f32[16,8,2,128,256]{4,3,2,1,0:T(8,128)} fusion(f32[4,8,2,128,256]{4,3,2,1,0:T(8,128)} %collective-permute-done, s32[1024]{0:T(1024)S(1)} %pad_clamp_fusion.8), kind=kCustom, calls=%fused_computation.4.clone.clone.1 | custom fusion | bytes 67108928 | tf_op jit(solution)/shard_map/while/body/eval_jaxpr/jit(_take)/gather | solution.py:44
  420.1 71.3 %fusion.84 = f32[16,8,2,128,128]{4,3,2,1,0:T(8,128)} fusion(f32[16,8,2,128,256]{4,3,2,1,0:T(8,128)} %gather_fusion, pred[16]{0:T(512)(128)(4,1)S(1)} %get-tuple-element.371, f32[16,8,1,2,128,256]{5,4,3,2,1,0:T(8,128)} %maximum_bitcast_fusion.4, f32[16,8,1,2,128,256]{5,4,3,2,1,0:T(8,128)} %fusion.83), kind=kOutput, calls=%fused_computation.19.clone.3 | convolution fusion | flops 25794969600 | bytes 117440528 | tf_op jit(solution)/shard_map/while/body/eval_jaxpr/gcokps,gckqs->gcopq/dot_general | solution.py:19
  491.4 17.7 %copy.35 = f32[16,8,2,128,128]{3,4,2,1,0:T(8,128)} copy(f32[16,8,2,128,128]{4,3,2,1,0:T(8,128)} %fusion.84) | data formatting | bytes 33554432 | tf_op jit(solution)/shard_map/while/body/eval_jaxpr/gcokps,gckqs->gcopq/dot_general | solution.py:19
  509.1 17.0 %fusion.85 = f32[66,8,2,128,128]{4,3,2,1,0:T(8,128)} fusion(f32[66,8,2,128,128]{4,3,2,1,0:T(8,128)} %get-tuple-element.390, s32[]{:T(128)S(6)} %select_n.381, f32[16,8,2,128,128]{4,3,2,1,0:T(8,128)} %fusion.84, f32[16,8,2,128,128]{3,4,2,1,0:T(8,128)} %copy.35, f32[2]{0:T(128)S(1)} %copy-done.6, pred[16]{0:T(512)(128)(4,1)S(1)} %copy-done.2), kind=kLoop, calls=%fused_computation.15.clone.1 | loop fusion | flops 12582912 | bytes 50331676 | tf_op jit(solution)/shard_map/while/body/eval_jaxpr/dynamic_update_slice | solution.py:51
  526.1 7.7 copy.44
  533.8 1.6 collective-permute-start
  536.0 16.3 %gather_fusion.1 = f32[16,8,2,128,256]{4,3,2,1,0:T(8,128)} fusion(f32[4,8,2,128,256]{4,3,2,1,0:T(8,128)} %get-tuple-element.405, s32[1024]{0:T(1024)S(1)} %pad_clamp_fusion.9), kind=kCustom, calls=%fused_computation.1.clone.clone.1 | custom fusion | bytes 67108928 | tf_op jit(solution)/shard_map/while/body/eval_jaxpr/jit(_take)/gather | solution.py:44
  552.3 23.4 %broadcast_select_fusion.5 = f32[16,8,2,128,256]{4,3,2,1,0:T(8,128)} fusion(f32[16,8,2,128,256]{4,3,2,1,0:T(8,128)} %gather_fusion.1, pred[16]{0:T(512)(128)(4,1)S(1)} %get-tuple-element.373), kind=kLoop, calls=%fused_computation.17.clone.2 | loop fusion | flops 8388608 | bytes 67108880 | tf_op jit(solution)/shard_map/while/body/eval_jaxpr/jit(_take)/select_n | solution.py:44
  575.7 21.4 %fusion.82 = (f32[16,8,1,128,256]{4,3,2,1,0:T(8,128)}, f32[16,8,1,128,256]{4,3,2,1,0:T(8,128)}) fusion(f32[16,8,2,128,256]{4,3,2,1,0:T(8,128)} %broadcast_select_fusion.5), kind=kLoop, calls=%fused_computation.133.clone.1 | loop fusion | flops 4194304 | bytes 67108864 | tf_op jit(solution)/shard_map/while/body/eval_jaxpr/slice | solution.py:17
  597.2 26.8 %maximum_bitcast_fusion.4 = f32[16,8,1,2,128,256]{5,4,3,2,1,0:T(8,128)} fusion(f32[16,8,1,128,256]{4,3,2,1,0:T(8,128)} %get-tuple-element.374, f32[16,8,1,128,256]{4,3,2,1,0:T(8,128)} %get-tuple-element.375), kind=kLoop, calls=%fused_computation.10.clone.1 | loop fusion | flops 8388608 | bytes 67108864 | tf_op jit(solution)/shard_map/while/body/eval_jaxpr/stack | solution.py:18
  624.0 1.5 slice-done.4
  625.5 1.2 slice-done.5
  627.9 1.2 slice-done.7
  629.1 11.3 fusion.83
  640.4 16.3 %gather_fusion = f32[16,8,2,128,256]{4,3,2,1,0:T(8,128)} fusion(f32[4,8,2,128,256]{4,3,2,1,0:T(8,128)} %collective-permute-done, s32[1024]{0:T(1024)S(1)} %pad_clamp_fusion.8), kind=kCustom, calls=%fused_computation.4.clone.clone.1 | custom fusion | bytes 67108928 | tf_op jit(solution)/shard_map/while/body/eval_jaxpr/jit(_take)/gather | solution.py:44
  656.8 71.3 %fusion.84 = f32[16,8,2,128,128]{4,3,2,1,0:T(8,128)} fusion(f32[16,8,2,128,256]{4,3,2,1,0:T(8,128)} %gather_fusion, pred[16]{0:T(512)(128)(4,1)S(1)} %get-tuple-element.371, f32[16,8,1,2,128,256]{5,4,3,2,1,0:T(8,128)} %maximum_bitcast_fusion.4, f32[16,8,1,2,128,256]{5,4,3,2,1,0:T(8,128)} %fusion.83), kind=kOutput, calls=%fused_computation.19.clone.3 | convolution fusion | flops 25794969600 | bytes 117440528 | tf_op jit(solution)/shard_map/while/body/eval_jaxpr/gcokps,gckqs->gcopq/dot_general | solution.py:19
  728.1 17.7 %copy.35 = f32[16,8,2,128,128]{3,4,2,1,0:T(8,128)} copy(f32[16,8,2,128,128]{4,3,2,1,0:T(8,128)} %fusion.84) | data formatting | bytes 33554432 | tf_op jit(solution)/shard_map/while/body/eval_jaxpr/gcokps,gckqs->gcopq/dot_general | solution.py:19
  745.7 17.0 %fusion.85 = f32[66,8,2,128,128]{4,3,2,1,0:T(8,128)} fusion(f32[66,8,2,128,128]{4,3,2,1,0:T(8,128)} %get-tuple-element.390, s32[]{:T(128)S(6)} %select_n.381, f32[16,8,2,128,128]{4,3,2,1,0:T(8,128)} %fusion.84, f32[16,8,2,128,128]{3,4,2,1,0:T(8,128)} %copy.35, f32[2]{0:T(128)S(1)} %copy-done.6, pred[16]{0:T(512)(128)(4,1)S(1)} %copy-done.2), kind=kLoop, calls=%fused_computation.15.clone.1 | loop fusion | flops 12582912 | bytes 50331676 | tf_op jit(solution)/shard_map/while/body/eval_jaxpr/dynamic_update_slice | solution.py:51
  762.7 7.7 copy.44
  771.2 16.3 %gather_fusion.1 = f32[16,8,2,128,256]{4,3,2,1,0:T(8,128)} fusion(f32[4,8,2,128,256]{4,3,2,1,0:T(8,128)} %get-tuple-element.405, s32[1024]{0:T(1024)S(1)} %pad_clamp_fusion.9), kind=kCustom, calls=%fused_computation.1.clone.clone.1 | custom fusion | bytes 67108928 | tf_op jit(solution)/shard_map/while/body/eval_jaxpr/jit(_take)/gather | solution.py:44
  787.5 23.4 %broadcast_select_fusion.5 = f32[16,8,2,128,256]{4,3,2,1,0:T(8,128)} fusion(f32[16,8,2,128,256]{4,3,2,1,0:T(8,128)} %gather_fusion.1, pred[16]{0:T(512)(128)(4,1)S(1)} %get-tuple-element.373), kind=kLoop, calls=%fused_computation.17.clone.2 | loop fusion | flops 8388608 | bytes 67108880 | tf_op jit(solution)/shard_map/while/body/eval_jaxpr/jit(_take)/select_n | solution.py:44
  810.9 21.4 %fusion.82 = (f32[16,8,1,128,256]{4,3,2,1,0:T(8,128)}, f32[16,8,1,128,256]{4,3,2,1,0:T(8,128)}) fusion(f32[16,8,2,128,256]{4,3,2,1,0:T(8,128)} %broadcast_select_fusion.5), kind=kLoop, calls=%fused_computation.133.clone.1 | loop fusion | flops 4194304 | bytes 67108864 | tf_op jit(solution)/shard_map/while/body/eval_jaxpr/slice | solution.py:17
  832.4 26.8 %maximum_bitcast_fusion.4 = f32[16,8,1,2,128,256]{5,4,3,2,1,0:T(8,128)} fusion(f32[16,8,1,128,256]{4,3,2,1,0:T(8,128)} %get-tuple-element.374, f32[16,8,1,128,256]{4,3,2,1,0:T(8,128)} %get-tuple-element.375), kind=kLoop, calls=%fused_computation.10.clone.1 | loop fusion | flops 8388608 | bytes 67108864 | tf_op jit(solution)/shard_map/while/body/eval_jaxpr/stack | solution.py:18
  859.2 1.5 slice-done.4
  864.3 11.3 fusion.83
  875.6 16.3 %gather_fusion = f32[16,8,2,128,256]{4,3,2,1,0:T(8,128)} fusion(f32[4,8,2,128,256]{4,3,2,1,0:T(8,128)} %collective-permute-done, s32[1024]{0:T(1024)S(1)} %pad_clamp_fusion.8), kind=kCustom, calls=%fused_computation.4.clone.clone.1 | custom fusion | bytes 67108928 | tf_op jit(solution)/shard_map/while/body/eval_jaxpr/jit(_take)/gather | solution.py:44
  892.0 71.3 %fusion.84 = f32[16,8,2,128,128]{4,3,2,1,0:T(8,128)} fusion(f32[16,8,2,128,256]{4,3,2,1,0:T(8,128)} %gather_fusion, pred[16]{0:T(512)(128)(4,1)S(1)} %get-tuple-element.371, f32[16,8,1,2,128,256]{5,4,3,2,1,0:T(8,128)} %maximum_bitcast_fusion.4, f32[16,8,1,2,128,256]{5,4,3,2,1,0:T(8,128)} %fusion.83), kind=kOutput, calls=%fused_computation.19.clone.3 | convolution fusion | flops 25794969600 | bytes 117440528 | tf_op jit(solution)/shard_map/while/body/eval_jaxpr/gcokps,gckqs->gcopq/dot_general | solution.py:19
  963.3 17.7 %copy.35 = f32[16,8,2,128,128]{3,4,2,1,0:T(8,128)} copy(f32[16,8,2,128,128]{4,3,2,1,0:T(8,128)} %fusion.84) | data formatting | bytes 33554432 | tf_op jit(solution)/shard_map/while/body/eval_jaxpr/gcokps,gckqs->gcopq/dot_general | solution.py:19
  980.9 17.0 %fusion.85 = f32[66,8,2,128,128]{4,3,2,1,0:T(8,128)} fusion(f32[66,8,2,128,128]{4,3,2,1,0:T(8,128)} %get-tuple-element.390, s32[]{:T(128)S(6)} %select_n.381, f32[16,8,2,128,128]{4,3,2,1,0:T(8,128)} %fusion.84, f32[16,8,2,128,128]{3,4,2,1,0:T(8,128)} %copy.35, f32[2]{0:T(128)S(1)} %copy-done.6, pred[16]{0:T(512)(128)(4,1)S(1)} %copy-done.2), kind=kLoop, calls=%fused_computation.15.clone.1 | loop fusion | flops 12582912 | bytes 50331676 | tf_op jit(solution)/shard_map/while/body/eval_jaxpr/dynamic_update_slice | solution.py:51
  997.9 7.7 copy.44
  1006.4 11.4 gather_fusion.4
  1017.8 11.9 %broadcast_select_fusion.2 = f32[8,8,2,128,256]{4,3,2,1,0:T(8,128)} fusion(f32[8,8,2,128,256]{4,3,2,1,0:T(8,128)} %gather_fusion.4, pred[8]{0:T(512)(128)(4,1)S(1)} %get-tuple-element.309), kind=kLoop, calls=%fused_computation.69 | loop fusion | flops 4194304 | bytes 33554440 | tf_op jit(solution)/shard_map/jit(_take)/select_n | solution.py:44
  1029.6 10.3 fusion.64
  1040.0 11.7 maximum_bitcast_fusion.2
  1051.7 6.2 fusion.66
  1057.9 39.5 %collective-permute-done.1 = f32[4,8,2,128,256]{4,3,2,1,0:T(8,128)} collective-permute-done((f32[4,8,2,128,256]{4,3,2,1,0:T(8,128)}, f32[4,8,2,128,256]{4,3,2,1,0:T(8,128)}, u32[]{:S(2)}, u32[]{:S(2)}) %collective-permute-start.1) | collective-permute-done | bytes 8388640 | tf_op jit(solution)/shard_map/ppermute | solution.py:10
  1097.4 11.0 gather_fusion.5
  1108.4 37.9 %fusion.41 = f32[8,8,2,128,128]{4,3,2,1,0:T(8,128)} fusion(f32[8,8,2,128,256]{4,3,2,1,0:T(8,128)} %gather_fusion.5, pred[8]{0:T(512)(128)(4,1)S(1)} %get-tuple-element.312, f32[8,8,1,2,128,256]{5,4,3,2,1,0:T(8,128)} %maximum_bitcast_fusion.2, f32[8,8,1,2,128,256]{5,4,3,2,1,0:T(8,128)} %fusion.66), kind=kOutput, calls=%fused_computation.72 | convolution fusion | flops 12897484800 | bytes 58720264 | tf_op jit(solution)/shard_map/gcokps,gckqs->gcopq/dot_general | solution.py:19
  1146.4 9.2 copy.27
  1155.5 12.1 %fusion.33 = f32[66,8,2,128,128]{4,3,2,1,0:T(8,128)} fusion(f32[66,8,2,128,128]{4,3,2,1,0:T(8,128)} %get-tuple-element.419, f32[8,8,2,128,128]{4,3,2,1,0:T(8,128)} %fusion.41, f32[8,8,2,128,128]{3,4,2,1,0:T(8,128)} %copy.27, f32[2]{0:T(128)S(1)} %copy-done.7, pred[8]{0:T(512)(128)(4,1)S(1)} %get-tuple-element.311), kind=kLoop, calls=%fused_computation.66 | loop fusion | flops 6291456 | bytes 25165840 | tf_op jit(solution)/shard_map/dynamic_update_slice | solution.py:51
  (121 shorter events, 11.6 us)
Async XLA Ops:
  0.0 14.2 %copy-start.3 = (s32[66,2]{0,1:T(2,128)S(1)}, s32[66,2]{0,1:T(2,128)}, u32[]{:S(2)}) copy-start(s32[66,2]{0,1:T(2,128)} %param.13) | copy-start | bytes 1588
  0.0 14.3 %copy-start.8 = (s32[64]{0:T(128)S(1)}, s32[64]{0:T(128)}, u32[]{:S(2)}) copy-start(s32[64]{0:T(128)} %param.14) | copy-start | bytes 772
  8.5 99.5 %all-to-all-start = ((f32[4,32,2,32,256]{4,3,2,0,1:T(8,128)}), f32[4,32,2,32,256]{4,3,2,0,1:T(8,128)}, u32[]{:S(2)}, u32[]{:S(2)}) async-start(f32[4,32,2,32,256]{4,3,2,0,1:T(8,128)} %copy.22), calls=%async_computation | async-start | bytes 16777216 | tf_op jit(solution)/shard_map/all_to_all | solution.py:24
  146.7 16.8 %copy-start = (f32[4,8,2,128,256]{4,3,2,1,0:T(8,128)S(1)}, f32[4,8,2,128,256]{4,3,2,1,0:T(8,128)}, u32[]{:S(2)}) copy-start(f32[4,8,2,128,256]{4,3,2,1,0:T(8,128)} %bitcast_multiply_fusion) | copy-start | bytes 25165828
  254.3 11.3 copy-start.5
  296.1 107.8 %collective-permute-start = (f32[4,8,2,128,256]{4,3,2,1,0:T(8,128)}, f32[4,8,2,128,256]{4,3,2,1,0:T(8,128)}, u32[]{:S(2)}, u32[]{:S(2)}) collective-permute-start(f32[4,8,2,128,256]{4,3,2,1,0:T(8,128)} %get-tuple-element.389), channel_id=1, source_target_pairs={{0,7},{1,0},{2,1},{3,2},{4,3},{5,4},{6,5},{7,6},{8,15},{9,8},{10,9... | collective-permute-start | bytes 25165832 | tf_op jit(solution)/shard_map/while/body/eval_jaxpr/ppermute | solution.py:10
  298.8 0.6 copy-start.1
  360.6 26.8 %slice-start = ((s8[33554432]{0:T(1024)(128)(4,1)}), s8[4194304]{0:T(1024)(128)(4,1)S(1)}, s32[]{:S(2)}) async-start(s8[33554432]{0:T(1024)(128)(4,1)} %bitcast.150), calls=%async_computation.1 | async-start | bytes 8388608 | tf_op jit(solution)/shard_map/while
  360.6 26.8 %slice-start.1 = ((s8[33554432]{0:T(1024)(128)(4,1)}), s8[4194304]{0:T(1024)(128)(4,1)S(1)}, s32[]{:S(2)}) async-start(s8[33554432]{0:T(1024)(128)(4,1)} %bitcast.150), calls=%async_computation.2 | async-start | bytes 8388608 | tf_op jit(solution)/shard_map/while
  360.6 26.8 %slice-start.2 = ((s8[33554432]{0:T(1024)(128)(4,1)}), s8[4194304]{0:T(1024)(128)(4,1)S(1)}, s32[]{:S(2)}) async-start(s8[33554432]{0:T(1024)(128)(4,1)} %bitcast.150), calls=%async_computation.3 | async-start | bytes 8388608 | tf_op jit(solution)/shard_map/while
  360.6 26.8 %slice-start.3 = ((s8[33554432]{0:T(1024)(128)(4,1)}), s8[4194304]{0:T(1024)(128)(4,1)S(1)}, s32[]{:S(2)}) async-start(s8[33554432]{0:T(1024)(128)(4,1)} %bitcast.150), calls=%async_computation.4 | async-start | bytes 8388608 | tf_op jit(solution)/shard_map/while
  360.6 28.4 %slice-start.4 = ((s8[33554432]{0:T(1024)(128)(4,1)}), s8[4194304]{0:T(1024)(128)(4,1)S(1)}, s32[]{:S(2)}) async-start(s8[33554432]{0:T(1024)(128)(4,1)} %bitcast.150), calls=%async_computation.5 | async-start | bytes 8388608 | tf_op jit(solution)/shard_map/while
  360.6 29.5 %slice-start.5 = ((s8[33554432]{0:T(1024)(128)(4,1)}), s8[4194304]{0:T(1024)(128)(4,1)S(1)}, s32[]{:S(2)}) async-start(s8[33554432]{0:T(1024)(128)(4,1)} %bitcast.150), calls=%async_computation.6 | async-start | bytes 8388608 | tf_op jit(solution)/shard_map/while
  360.7 30.7 %slice-start.6 = ((s8[33554432]{0:T(1024)(128)(4,1)}), s8[4194304]{0:T(1024)(128)(4,1)S(1)}, s32[]{:S(2)}) async-start(s8[33554432]{0:T(1024)(128)(4,1)} %bitcast.150), calls=%async_computation.7 | async-start | bytes 8388608 | tf_op jit(solution)/shard_map/while
  360.7 31.9 %slice-start.7 = ((s8[33554432]{0:T(1024)(128)(4,1)}), s8[4194304]{0:T(1024)(128)(4,1)S(1)}, s32[]{:S(2)}) async-start(s8[33554432]{0:T(1024)(128)(4,1)} %bitcast.150), calls=%async_computation.8 | async-start | bytes 8388608 | tf_op jit(solution)/shard_map/while
  491.4 17.7 %copy-start.2 = (pred[16]{0:T(512)(128)(4,1)S(1)}, pred[16]{0:T(512)(128)(4,1)}, u32[]{:S(2)}) copy-start(pred[16]{0:T(512)(128)(4,1)} %copy-done.1) | copy-start | bytes 52 | tf_op jit(solution)/shard_map/while
  491.4 17.7 %copy-start.6 = (f32[2]{0:T(128)S(1)}, f32[2]{0:T(128)}, u32[]{:S(2)}) copy-start(f32[2]{0:T(128)} %get-tuple-element.411) | copy-start | bytes 28 | tf_op jit(solution)/shard_map/while
  526.1 7.7 copy-start.4
  533.8 106.7 %collective-permute-start = (f32[4,8,2,128,256]{4,3,2,1,0:T(8,128)}, f32[4,8,2,128,256]{4,3,2,1,0:T(8,128)}, u32[]{:S(2)}, u32[]{:S(2)}) collective-permute-start(f32[4,8,2,128,256]{4,3,2,1,0:T(8,128)} %get-tuple-element.389), channel_id=1, source_target_pairs={{0,7},{1,0},{2,1},{3,2},{4,3},{5,4},{6,5},{7,6},{8,15},{9,8},{10,9... | collective-permute-start | bytes 25165832 | tf_op jit(solution)/shard_map/while/body/eval_jaxpr/ppermute | solution.py:10
  535.5 0.6 copy-start.1
  597.1 26.8 %slice-start = ((s8[33554432]{0:T(1024)(128)(4,1)}), s8[4194304]{0:T(1024)(128)(4,1)S(1)}, s32[]{:S(2)}) async-start(s8[33554432]{0:T(1024)(128)(4,1)} %bitcast.150), calls=%async_computation.1 | async-start | bytes 8388608 | tf_op jit(solution)/shard_map/while
  597.1 26.8 %slice-start.1 = ((s8[33554432]{0:T(1024)(128)(4,1)}), s8[4194304]{0:T(1024)(128)(4,1)S(1)}, s32[]{:S(2)}) async-start(s8[33554432]{0:T(1024)(128)(4,1)} %bitcast.150), calls=%async_computation.2 | async-start | bytes 8388608 | tf_op jit(solution)/shard_map/while
  597.1 26.8 %slice-start.2 = ((s8[33554432]{0:T(1024)(128)(4,1)}), s8[4194304]{0:T(1024)(128)(4,1)S(1)}, s32[]{:S(2)}) async-start(s8[33554432]{0:T(1024)(128)(4,1)} %bitcast.150), calls=%async_computation.3 | async-start | bytes 8388608 | tf_op jit(solution)/shard_map/while
  597.1 26.8 %slice-start.3 = ((s8[33554432]{0:T(1024)(128)(4,1)}), s8[4194304]{0:T(1024)(128)(4,1)S(1)}, s32[]{:S(2)}) async-start(s8[33554432]{0:T(1024)(128)(4,1)} %bitcast.150), calls=%async_computation.4 | async-start | bytes 8388608 | tf_op jit(solution)/shard_map/while
  597.2 28.4 %slice-start.4 = ((s8[33554432]{0:T(1024)(128)(4,1)}), s8[4194304]{0:T(1024)(128)(4,1)S(1)}, s32[]{:S(2)}) async-start(s8[33554432]{0:T(1024)(128)(4,1)} %bitcast.150), calls=%async_computation.5 | async-start | bytes 8388608 | tf_op jit(solution)/shard_map/while
  597.2 29.5 %slice-start.5 = ((s8[33554432]{0:T(1024)(128)(4,1)}), s8[4194304]{0:T(1024)(128)(4,1)S(1)}, s32[]{:S(2)}) async-start(s8[33554432]{0:T(1024)(128)(4,1)} %bitcast.150), calls=%async_computation.6 | async-start | bytes 8388608 | tf_op jit(solution)/shard_map/while
  597.2 30.7 %slice-start.6 = ((s8[33554432]{0:T(1024)(128)(4,1)}), s8[4194304]{0:T(1024)(128)(4,1)S(1)}, s32[]{:S(2)}) async-start(s8[33554432]{0:T(1024)(128)(4,1)} %bitcast.150), calls=%async_computation.7 | async-start | bytes 8388608 | tf_op jit(solution)/shard_map/while
  597.2 31.9 %slice-start.7 = ((s8[33554432]{0:T(1024)(128)(4,1)}), s8[4194304]{0:T(1024)(128)(4,1)S(1)}, s32[]{:S(2)}) async-start(s8[33554432]{0:T(1024)(128)(4,1)} %bitcast.150), calls=%async_computation.8 | async-start | bytes 8388608 | tf_op jit(solution)/shard_map/while
  728.1 17.7 %copy-start.2 = (pred[16]{0:T(512)(128)(4,1)S(1)}, pred[16]{0:T(512)(128)(4,1)}, u32[]{:S(2)}) copy-start(pred[16]{0:T(512)(128)(4,1)} %copy-done.1) | copy-start | bytes 52 | tf_op jit(solution)/shard_map/while
  728.1 17.7 %copy-start.6 = (f32[2]{0:T(128)S(1)}, f32[2]{0:T(128)}, u32[]{:S(2)}) copy-start(f32[2]{0:T(128)} %get-tuple-element.411) | copy-start | bytes 28 | tf_op jit(solution)/shard_map/while
  762.7 7.7 copy-start.4
  770.4 105.2 %collective-permute-start = (f32[4,8,2,128,256]{4,3,2,1,0:T(8,128)}, f32[4,8,2,128,256]{4,3,2,1,0:T(8,128)}, u32[]{:S(2)}, u32[]{:S(2)}) collective-permute-start(f32[4,8,2,128,256]{4,3,2,1,0:T(8,128)} %get-tuple-element.389), channel_id=1, source_target_pairs={{0,7},{1,0},{2,1},{3,2},{4,3},{5,4},{6,5},{7,6},{8,15},{9,8},{10,9... | collective-permute-start | bytes 25165832 | tf_op jit(solution)/shard_map/while/body/eval_jaxpr/ppermute | solution.py:10
  770.6 0.6 copy-start.1
  832.3 26.8 %slice-start = ((s8[33554432]{0:T(1024)(128)(4,1)}), s8[4194304]{0:T(1024)(128)(4,1)S(1)}, s32[]{:S(2)}) async-start(s8[33554432]{0:T(1024)(128)(4,1)} %bitcast.150), calls=%async_computation.1 | async-start | bytes 8388608 | tf_op jit(solution)/shard_map/while
  832.3 26.8 %slice-start.1 = ((s8[33554432]{0:T(1024)(128)(4,1)}), s8[4194304]{0:T(1024)(128)(4,1)S(1)}, s32[]{:S(2)}) async-start(s8[33554432]{0:T(1024)(128)(4,1)} %bitcast.150), calls=%async_computation.2 | async-start | bytes 8388608 | tf_op jit(solution)/shard_map/while
  832.3 26.8 %slice-start.2 = ((s8[33554432]{0:T(1024)(128)(4,1)}), s8[4194304]{0:T(1024)(128)(4,1)S(1)}, s32[]{:S(2)}) async-start(s8[33554432]{0:T(1024)(128)(4,1)} %bitcast.150), calls=%async_computation.3 | async-start | bytes 8388608 | tf_op jit(solution)/shard_map/while
  832.3 26.8 %slice-start.3 = ((s8[33554432]{0:T(1024)(128)(4,1)}), s8[4194304]{0:T(1024)(128)(4,1)S(1)}, s32[]{:S(2)}) async-start(s8[33554432]{0:T(1024)(128)(4,1)} %bitcast.150), calls=%async_computation.4 | async-start | bytes 8388608 | tf_op jit(solution)/shard_map/while
  832.4 28.4 %slice-start.4 = ((s8[33554432]{0:T(1024)(128)(4,1)}), s8[4194304]{0:T(1024)(128)(4,1)S(1)}, s32[]{:S(2)}) async-start(s8[33554432]{0:T(1024)(128)(4,1)} %bitcast.150), calls=%async_computation.5 | async-start | bytes 8388608 | tf_op jit(solution)/shard_map/while
  832.4 29.5 %slice-start.5 = ((s8[33554432]{0:T(1024)(128)(4,1)}), s8[4194304]{0:T(1024)(128)(4,1)S(1)}, s32[]{:S(2)}) async-start(s8[33554432]{0:T(1024)(128)(4,1)} %bitcast.150), calls=%async_computation.6 | async-start | bytes 8388608 | tf_op jit(solution)/shard_map/while
  832.4 30.7 %slice-start.6 = ((s8[33554432]{0:T(1024)(128)(4,1)}), s8[4194304]{0:T(1024)(128)(4,1)S(1)}, s32[]{:S(2)}) async-start(s8[33554432]{0:T(1024)(128)(4,1)} %bitcast.150), calls=%async_computation.7 | async-start | bytes 8388608 | tf_op jit(solution)/shard_map/while
  832.4 31.9 %slice-start.7 = ((s8[33554432]{0:T(1024)(128)(4,1)}), s8[4194304]{0:T(1024)(128)(4,1)S(1)}, s32[]{:S(2)}) async-start(s8[33554432]{0:T(1024)(128)(4,1)} %bitcast.150), calls=%async_computation.8 | async-start | bytes 8388608 | tf_op jit(solution)/shard_map/while
  963.3 17.7 %copy-start.2 = (pred[16]{0:T(512)(128)(4,1)S(1)}, pred[16]{0:T(512)(128)(4,1)}, u32[]{:S(2)}) copy-start(pred[16]{0:T(512)(128)(4,1)} %copy-done.1) | copy-start | bytes 52 | tf_op jit(solution)/shard_map/while
  963.3 17.7 %copy-start.6 = (f32[2]{0:T(128)S(1)}, f32[2]{0:T(128)}, u32[]{:S(2)}) copy-start(f32[2]{0:T(128)} %get-tuple-element.411) | copy-start | bytes 28 | tf_op jit(solution)/shard_map/while
  997.9 7.7 copy-start.4
  1005.6 91.8 %collective-permute-start.1 = (f32[4,8,2,128,256]{4,3,2,1,0:T(8,128)}, f32[4,8,2,128,256]{4,3,2,1,0:T(8,128)}, u32[]{:S(2)}, u32[]{:S(2)}) collective-permute-start(f32[4,8,2,128,256]{4,3,2,1,0:T(8,128)} %get-tuple-element.418), channel_id=1, source_target_pairs={{0,7},{1,0},{2,1},{3,2},{4,3},{5,4},{6,5},{7,6},{8,15},{9,8},{10,9... | collective-permute-start | bytes 25165832 | tf_op jit(solution)/shard_map/ppermute | solution.py:10
  1029.6 22.0 %slice-start.8 = ((s8[16777216]{0:T(1024)(128)(4,1)}), s8[4194304]{0:T(1024)(128)(4,1)S(1)}, s32[]{:S(2)}) async-start(s8[16777216]{0:T(1024)(128)(4,1)} %bitcast.152), calls=%async_computation.9 | async-start | bytes 8388608
  1029.6 22.0 %slice-start.9 = ((s8[16777216]{0:T(1024)(128)(4,1)}), s8[4194304]{0:T(1024)(128)(4,1)S(1)}, s32[]{:S(2)}) async-start(s8[16777216]{0:T(1024)(128)(4,1)} %bitcast.152), calls=%async_computation.10 | async-start | bytes 8388608
  1040.0 11.7 %slice-start.10 = ((s8[16777216]{0:T(1024)(128)(4,1)}), s8[4194304]{0:T(1024)(128)(4,1)S(1)}, s32[]{:S(2)}) async-start(s8[16777216]{0:T(1024)(128)(4,1)} %bitcast.152), calls=%async_computation.11 | async-start | bytes 8388608
  1040.0 11.7 %slice-start.11 = ((s8[16777216]{0:T(1024)(128)(4,1)}), s8[4194304]{0:T(1024)(128)(4,1)S(1)}, s32[]{:S(2)}) async-start(s8[16777216]{0:T(1024)(128)(4,1)} %bitcast.152), calls=%async_computation.12 | async-start | bytes 8388608
  1146.4 9.2 copy-start.7
where the time goes:
time: 1170 us
  other arithmetic  429 us (37%)
  local copies, waits for them, and re-layouts  298 us (25%)
  matrix products  296 us (25%)
  waiting for transfers between devices  133 us (11%)
    dot_general x5, matrix products, correlate(): jnp.einsum('gcokps,gckqs->gcopq', stacked, right, precision=prec) * scale  296 us
    another operation x10, other arithmetic, correlate(): jnp.stack([jnp.stack([left_re, left_im], 2), jnp.stack([left_im, -left_re...  165 us
    select_n x5, other arithmetic, correlate_group(): jnp.take(own_blocks, own_local, axis=0)  98.5 us
    all_to_all x1, waiting for transfers between devices, shards(): lax.all_to_all(voltages, 'freq', split_axis=1, concat_axis=3, tiled=True)  93.6 us
    slice x5, other arithmetic, correlate(): left_im = left[:, :, 1]  88.5 us
    dot_general x5, local copies, waits for them, and re-layouts, correlate(): jnp.einsum('gcokps,gckqs->gcopq', stacked, right, precision=prec) * scale  73.4 us
    gather x5, local copies, waits for them, and re-layouts, correlate_group(): jnp.take(own_blocks, own_local, axis=0)  73.1 us
    gather x5, local copies, waits for them, and re-layouts, correlate_group(): jnp.take(far_blocks, far_local, axis=0)  72.8 us
  transfers between devices with their start and end apart: 5, of which 2 were waited for; matrix products, arithmetic and copies ran while one was open for 30% of the time, Pallas kernels for 0%

commit v1 on v0

v1 whole, which is shorter than its diff:
```python
import functools

import jax
import jax.numpy as jnp
from jax import lax
from jax.experimental import pallas as pl
from jax.experimental.pallas import tpu as pltpu
from jax.sharding import PartitionSpec as P


def passed_along(value, axis):
    count = lax.axis_size(axis)
    pairs = [(source, (source - 1) % count) for source in range(count)]
    return lax.ppermute(value, axis, pairs)


def turned(value):
    return lax.all_to_all(value, "freq", split_axis=0, concat_axis=0, tiled=True)


def tiles_kernel(start, count, chan0, steps, n_sets, has_prev, slots_ref, *refs):
    sets = refs[:n_sets]
    out_ref, hi, lo, stage, sems = refs[n_sets + has_prev :]
    step = pl.program_id(0)
    slot = lax.rem(step, 2)
    groups, per_dev, _, rows, samples = sets[0].shape
    width = groups * rows
    scale = 1.0 / samples

    def copy_out(which, channel):
        return pltpu.make_async_copy(
            stage.at[which],
            out_ref.at[pl.ds(start, count), chan0 + channel],
            sems.at[which],
        )

    for index, ref in enumerate(sets):
        for block in range(per_dev):
            at = index * per_dev + block
            re = ref[:, block, 0].reshape(width, samples)
            im = ref[:, block, 1].reshape(width, samples)
            re_hi = re.astype(jnp.bfloat16)
            im_hi = im.astype(jnp.bfloat16)
            re_rest = re - re_hi.astype(jnp.float32)
            im_rest = im - im_hi.astype(jnp.float32)
            for held, real, imag, minus in (
                (hi, re_hi, im_hi, (-im).astype(jnp.bfloat16)),
                (
                    lo,
                    re_rest.astype(jnp.bfloat16),
                    im_rest.astype(jnp.bfloat16),
                    (-im_rest).astype(jnp.bfloat16),
                ),
            ):
                held[at, :width, :samples] = real
                held[at, :width, samples:] = imag
                held[at, width:, :samples] = minus
                held[at, width:, samples:] = real

    if steps > 2:

        @pl.when(step >= 2)
        def _():
            copy_out(slot, step - 2).wait()

    def dot(a, b):
        return lax.dot_general(
            a, b, (((1,), (1,)), ((), ())), preferred_element_type=jnp.float32
        )

    def tile(index, carry):
        x = slots_ref[2 * (start + index)]
        y = slots_ref[2 * (start + index) + 1]
        x_hi = hi[x, :width, :]
        x_lo = lo[x, :width, :]
        y_hi = hi[y]
        y_lo = lo[y]
        total = (dot(x_lo, y_hi) + dot(x_hi, y_lo) + dot(x_hi, y_hi)) * scale
        stage[slot, index, 0] = total[:, :width]
        stage[slot, index, 1] = total[:, width:]
        return carry

    lax.fori_loop(0, count, tile, 0, unroll=2 if count % 2 == 0 else 1)
    copy_out(slot, step).start()

    @pl.when(step == steps - 1)
    def _():
        if steps > 1:
            copy_out(lax.rem(step + 1, 2), step - 1).wait()
        copy_out(slot, step).wait()


def place_group(prev, out_type, slots, start, count, chan0, sets):
    groups, per_dev, steps, _, rows, samples = sets[0].shape
    width = groups * rows
    n_sets = len(sets)
    has_prev = 0 if prev is None else 1
    spec = pl.BlockSpec(
        (groups, per_dev, None, 2, rows, samples), lambda c, *_: (0, 0, c, 0, 0, 0)
    )
    any_spec = pl.BlockSpec(memory_space=pl.ANY)
    flops = 3 * 2 * 2 * width * width * 2 * samples * count * steps
    moved = 4 * (sum(one.size for one in sets) + 2 * width * width * count * steps)
    call = pl.pallas_call(
        functools.partial(tiles_kernel, start, count, chan0, steps, n_sets, has_prev),
        out_shape=out_type,
        grid_spec=pltpu.PrefetchScalarGridSpec(
            num_scalar_prefetch=1,
            grid=(steps,),
            in_specs=[spec] * n_sets + [any_spec] * has_prev,
            out_specs=any_spec,
            scratch_shapes=[
                pltpu.VMEM((n_sets * per_dev, 2 * width, 2 * samples), jnp.bfloat16),
                pltpu.VMEM((n_sets * per_dev, 2 * width, 2 * samples), jnp.bfloat16),
                pltpu.VMEM((2, count, 2, width, width), jnp.float32),
                pltpu.SemaphoreType.DMA((2,)),
            ],
        ),
        input_output_aliases={1 + n_sets: 0} if has_prev else {},
        compiler_params=pltpu.CompilerParams(
            dimension_semantics=("arbitrary",), vmem_limit_bytes=32 * 1024 * 1024
        ),
        cost_estimate=pl.CostEstimate(
            flops=flops, bytes_accessed=moved, transcendentals=0
        ),
    )
    return call(slots, *sets, *([prev] if has_prev else []))


def shards(voltages, pair_table, bad_feeds):
    blk_count = lax.axis_size("blk")
    freq_count = lax.axis_size("freq")
    here = lax.axis_index("blk")
    per_dev, chans, _, rows, samples = voltages.shape
    width = rows * freq_count
    chan_dev = chans // freq_count
    half = blk_count // 2
    chunks = 4 if per_dev > 1 and chan_dev % 4 == 0 else 1
    per_chunk = chan_dev // chunks
    tile_count = per_dev * per_dev
    own_count = per_dev * (per_dev + 1) // 2
    shared_count = (tile_count + 1) // 2

    blocks = here * per_dev + jnp.arange(per_dev, dtype=jnp.int32)
    places = lax.axis_index("freq") * rows + jnp.arange(rows, dtype=jnp.int32)
    inputs = blocks[:, None] * width + places[None, :]
    flagged = jnp.any((inputs // 2)[:, :, None] == bad_feeds[None, None, :], axis=-1)
    keep = jnp.where(flagged, 0.0, 1.0).astype(jnp.float32)
    slots = jnp.where(
        pair_table // per_dev == here, pair_table % per_dev, per_dev + pair_table % per_dev
    ).reshape(-1)

    split = voltages.reshape(per_dev, freq_count, chunks, per_chunk, 2, rows, samples)
    raw = [
        jnp.swapaxes(split[:, :, g], 0, 1) * keep[None, :, None, None, :, None]
        for g in range(chunks)
    ]
    early = passed_along(raw[-1], "blk") if chunks > 1 else None
    own = [turned(piece) for piece in raw]

    out_type = jax.ShapeDtypeStruct(
        (pair_table.shape[0], chan_dev, 2, width, width), jnp.float32
    )
    visibility = None
    for g in range(chunks):
        visibility = place_group(
            visibility, out_type, slots, 0, own_count, g * per_chunk, [own[g]]
        )
    far = own
    for step in range(1, half + 1):
        far = [
            turned(early)
            if step == 1 and early is not None and g == chunks - 1
            else passed_along(far[g], "blk")
            for g in range(chunks)
        ]
        for g in range(chunks):
            visibility = place_group(
                visibility,
                out_type,
                slots,
                own_count + (step - 1) * tile_count,
                tile_count if step < half else shared_count,
                g * per_chunk,
                [own[g], far[g]],
            )
    return visibility


def solution(mesh):
    placed = (P("blk", None, None, "freq", None), P("blk", None), P())
    return jax.shard_map(
        shards,
        mesh=mesh,
        in_specs=placed,
        out_specs=P("blk", "freq", None, None, None),
        check_vma=False,
    )
```

time: 1170 us -> 493 us (0.42)
  other arithmetic: 429 us -> 6.71 us
  matrix products: 296 us -> 0 us
  local copies, waits for them, and re-layouts: 298 us -> 7.16 us
  Pallas kernels: 0 us -> 246 us
  blocking collectives: 0 us -> 57.7 us
  starting transfers between devices: 10.5 us -> 48.2 us
    dot_general x5 -> x0, matrix products: 296 us -> none  [correlate(): jnp.einsum('gcokps,gckqs->gcopq', stacked, right, precision=prec) * scale]
    pallas_call x0 -> x20, Pallas kernels: none -> 246 us  [place_group(): return call(slots, *sets, *([prev] if has_prev else []))]
    another operation x10 -> x0, other arithmetic: 165 us -> none  [correlate(): jnp.stack([jnp.stack([left_re, left_im], 2), jnp.stack([left_im, -left_re...]
    gather x10 -> x0, local copies, waits for them, and re-layouts: 146 us -> none  [the longest x5 73.1 us: correlate_group(): jnp.take(own_blocks, own_local, axis=0)]
    select_n x6 -> x1, other arithmetic: 107 us -> 0.02 us  [shards(): jnp.where(pair_table // per_dev == here, pair_table % per_dev, per_dev +...]
    slice x5 -> x0, other arithmetic: 88.5 us -> none  [correlate(): left_im = left[:, :, 1]]
    all_to_all x1 -> x3, waiting for transfers between devices: 93.6 us -> 18.4 us  [turned(): lax.all_to_all(value, 'freq', split_axis=0, concat_axis=0, tiled=True)]
    dot_general x5 -> x0, local copies, waits for them, and re-layouts: 73.4 us -> none  [correlate(): jnp.einsum('gcokps,gckqs->gcopq', stacked, right, precision=prec) * scale]
  transfers between devices with their start and end apart: 5 -> 19, of which waited for: 2 -> 8; matrix products, arithmetic and copies ran while one was open for 30% -> 0% of each run, Pallas kernels for 0% -> 48%
where the time goes in v1:
time: 493 us
  Pallas kernels  246 us (50%)
  waiting for transfers between devices  126 us (26%)
  blocking collectives  57.7 us (12%)
  starting transfers between devices  48.2 us (10%)
  local copies, waits for them, and re-layouts  7.16 us (1%)
  other arithmetic  6.71 us (1%)
    pallas_call x20, Pallas kernels, place_group(): return call(slots, *sets, *([prev] if has_prev else []))  246 us
    ppermute x16, waiting for transfers between devices, passed_along(): return lax.ppermute(value, axis, pairs)  108 us
    all_to_all x2, blocking collectives, turned(): lax.all_to_all(value, 'freq', split_axis=0, concat_axis=0, tiled=True)  57.7 us
    ppermute x16, starting transfers between devices, passed_along(): return lax.ppermute(value, axis, pairs)  34.8 us
    all_to_all x3, waiting for transfers between devices, turned(): lax.all_to_all(value, 'freq', split_axis=0, concat_axis=0, tiled=True)  18.4 us
    all_to_all x3, starting transfers between devices, turned(): lax.all_to_all(value, 'freq', split_axis=0, concat_axis=0, tiled=True)  13.4 us
  transfers between devices with their start and end apart: 19, of which 8 were waited for; matrix products, arithmetic and copies ran while one was open for 0% of the time, Pallas kernels for 48%

profile of v1, /device:TPU:0, one launch (start us, length us, event | category | flops | bytes accessed | tf_op | source)
XLA Modules:
  0.0 492.8 jit_solution(6481616450865536926)
XLA Ops:
  0.0 6.9 %fusion.11 = (f32[4,4,1,2,2,32,256]{6,5,4,3,2,1,0:T(8,128)S(1)}, f32[4,4,1,2,2,32,256]{6,5,4,3,2,1,0:T(8,128)}, f32[4,4,1,2,2,32,256]{6,5,4,3,2,1,0:T(8,128)}, f32[4,4,1,2,2,32,256]{6,5,4,3,2,1,0:T(8,128)}) fusion(f32[4,4,4,2,2,32,256]{6,5,4,3,2,1,0:T(8,128)} %bitcast.33), kind=kLoop, calls=%fused_computation.32 | loop fusion | bytes 16777216 | tf_op jit(solution)/shard_map/slice | solution.py:155
  6.9 0.1 add_select_fusion.1
  7.0 0.2 compare_reduce_fusion
  7.2 6.4 %fusion.1 = (f32[4,4,2,2,32,256]{5,4,3,2,1,0:T(8,128)S(1)}, f32[4,4,2,2,32,256]{5,4,3,2,1,0:T(8,128)}, f32[4,4,2,2,32,256]{5,4,3,2,1,0:T(8,128)S(1)}, f32[4,4,2,2,32,256]{5,4,3,2,1,0:T(8,128)}) fusion(f32[4,4,1,2,2,32,256]{6,5,4,3,2,1,0:T(8,128)S(1)} %get-tuple-element.5, f32[4,32]{1,0:T(4,128)S(1)} %broadcast_select_fusion, ...), kind=kLoop, calls=%fused_computation.2 | loop fusion | flops 2097152 | bytes 16777728 | tf_op jit(solution)/shard_map/mul | solution.py:155
  13.6 30.3 %all_to_all.25.refs_0_ = f32[4,4,2,2,32,256]{5,4,3,2,1,0:T(8,128)S(1)} all-to-all(f32[4,4,2,2,32,256]{5,4,3,2,1,0:T(8,128)S(1)} %get-tuple-element.9), channel_id=1, replica_groups=mesh['freq'=4,'blk'=8] {'freq'}, dimensions={0} | all-to-all | bytes 4194304 | tf_op jit(solution)/shard_map/all_to_all | solution.py:18
  43.9 27.4 %all_to_all.26.refs_0_ = f32[4,4,2,2,32,256]{5,4,3,2,1,0:T(8,128)} all-to-all(f32[4,4,2,2,32,256]{5,4,3,2,1,0:T(8,128)S(1)} %get-tuple-element.11), channel_id=1, replica_groups=mesh['freq'=4,'blk'=8] {'freq'}, dimensions={0} | all-to-all | bytes 4194304 | tf_op jit(solution)/shard_map/all_to_all | solution.py:18
  71.3 4.5 all-to-all-start.2
  75.8 0.1 collective-permute-start
  75.9 3.6 collective-permute-start.12
  79.6 0.1 collective-permute-start.8
  79.6 18.4 %all-to-all-done.2.refs_0_ = f32[4,4,2,2,32,256]{5,4,3,2,1,0:T(8,128)} async-done(((f32[4,4,2,2,32,256]{5,4,3,2,1,0:T(8,128)}), f32[4,4,2,2,32,256]{5,4,3,2,1,0:T(8,128)}, u32[]{:S(2)}, u32[]{:S(2)}) %all-to-all-start.2) | async-done | bytes 2097184 | tf_op jit(solution)/shard_map/all_to_all | solution.py:18
  98.0 2.2 collective-permute-start.4
  100.3 4.5 all-to-all-start.1
  104.8 0.0 copy-start.2
  104.8 17.4 %collective-permute-done.12.refs_1_ = f32[4,4,2,2,32,256]{5,4,3,2,1,0:T(8,128)} collective-permute-done((f32[4,4,2,2,32,256]{5,4,3,2,1,0:T(8,128)S(1)}, f32[4,4,2,2,32,256]{5,4,3,2,1,0:T(8,128)}, u32[]{:S(2)}, u32[]{:S(2)}) %collective-permute-start.12) | collective-permute-done | bytes 2097184 | tf_op jit(solution)/shard_map/ppermute | solution.py:14
  122.2 3.8 collective-permute-start.13
  126.0 18.8 %collective-permute-done.8.refs_1_ = f32[4,4,2,2,32,256]{5,4,3,2,1,0:T(8,128)} collective-permute-done((f32[4,4,2,2,32,256]{5,4,3,2,1,0:T(8,128)}, f32[4,4,2,2,32,256]{5,4,3,2,1,0:T(8,128)}, u32[]{:S(2)}, u32[]{:S(2)}) %collective-permute-start.8) | collective-permute-done | bytes 2097184 | tf_op jit(solution)/shard_map/ppermute | solution.py:14
  144.7 3.7 collective-permute-start.9
  148.4 18.8 %collective-permute-done.4.refs_1_ = f32[4,4,2,2,32,256]{5,4,3,2,1,0:T(8,128)} collective-permute-done((f32[4,4,2,2,32,256]{5,4,3,2,1,0:T(8,128)}, f32[4,4,2,2,32,256]{5,4,3,2,1,0:T(8,128)}, u32[]{:S(2)}, u32[]{:S(2)}) %collective-permute-start.4) | collective-permute-done | bytes 2097184 | tf_op jit(solution)/shard_map/ppermute | solution.py:14
  167.2 3.7 collective-permute-start.5
  170.9 0.0 all-to-all-done.1.refs_1_
  170.9 0.0 collective-permute-start.1
  171.0 4.4 all-to-all-start
  175.4 0.1 copy.28
  175.5 0.1 reshape.62.slots_ref
  175.7 14.0 %collective-permute-done.13.refs_1_ = f32[4,4,2,2,32,256]{5,4,3,2,1,0:T(8,128)} collective-permute-done((f32[4,4,2,2,32,256]{5,4,3,2,1,0:T(8,128)}, f32[4,4,2,2,32,256]{5,4,3,2,1,0:T(8,128)}, u32[]{:S(2)}, u32[]{:S(2)}) %collective-permute-start.13) | collective-permute-done | bytes 2097184 | tf_op jit(solution)/shard_map/ppermute | solution.py:14
  189.7 3.7 collective-permute-start.14
  193.4 18.8 %collective-permute-done.9.refs_1_ = f32[4,4,2,2,32,256]{5,4,3,2,1,0:T(8,128)} collective-permute-done((f32[4,4,2,2,32,256]{5,4,3,2,1,0:T(8,128)}, f32[4,4,2,2,32,256]{5,4,3,2,1,0:T(8,128)}, u32[]{:S(2)}, u32[]{:S(2)}) %collective-permute-start.9) | collective-permute-done | bytes 2097184 | tf_op jit(solution)/shard_map/ppermute | solution.py:14
  212.2 3.7 collective-permute-start.10
  215.9 8.7 %shard_map.37.refs_1_ = f32[66,8,2,128,128]{4,3,2,1,0:T(8,128)} custom-call(s32[132]{0:T(256)S(1)} %reshape.62.slots_ref, f32[4,4,2,2,32,256]{5,4,3,2,1,0:T(8,128)S(1)} %all_to_all.25.refs_0_), custom_call_target="tpu_custom_call" | custom-call | flops 2013265920 | bytes 4718592 | tf_op jit(solution)/shard_map/pallas_call | solution.py:127
  224.6 8.7 %shard_map.38.refs_1_ = f32[66,8,2,128,128]{4,3,2,1,0:T(8,128)} custom-call(s32[132]{0:T(256)S(1)} %reshape.62.slots_ref, f32[4,4,2,2,32,256]{5,4,3,2,1,0:T(8,128)S(1)} %copy-done, f32[66,8,2,128,128]{4,3,2,1,0:T(8,128)} %shard_map.37.refs_1_), custom_call_target="tpu_custom_call", output_to_operand_aliasing={{}: (2, {})} | custom-call | flops 2013265920 | bytes 4718592 | tf_op jit(solution)/shard_map/pallas_call | solution.py:127
  233.3 1.3 collective-permute-done.5.refs_1_
  234.6 3.7 collective-permute-start.6
  238.3 18.8 %collective-permute-done.1.refs_1_ = f32[4,4,2,2,32,256]{5,4,3,2,1,0:T(8,128)} collective-permute-done((f32[4,4,2,2,32,256]{5,4,3,2,1,0:T(8,128)}, f32[4,4,2,2,32,256]{5,4,3,2,1,0:T(8,128)}, u32[]{:S(2)}, u32[]{:S(2)}) %collective-permute-start.1) | collective-permute-done | bytes 2097184 | tf_op jit(solution)/shard_map/ppermute | solution.py:14
  257.1 3.7 collective-permute-start.2
  260.8 9.8 %shard_map.39.refs_1_ = f32[66,8,2,128,128]{4,3,2,1,0:T(8,128)} custom-call(s32[132]{0:T(256)S(1)} %reshape.62.slots_ref, f32[4,4,2,2,32,256]{5,4,3,2,1,0:T(8,128)} %all-to-all-done.2.refs_0_, f32[66,8,2,128,128]{4,3,2,1,0:T(8,128)} %shard_map.38.refs_1_), custom_call_target="tpu_custom_call", output_to_operand_aliasing={{}: (2, {})} | custom-call | flops 2013265920 | bytes 4718592 | tf_op jit(solution)/shard_map/pallas_call | solution.py:127
  270.6 0.0 all-to-all-done.refs_0_
  270.6 9.8 %shard_map.40.refs_2_ = f32[66,8,2,128,128]{4,3,2,1,0:T(8,128)} custom-call(s32[132]{0:T(256)S(1)} %reshape.62.slots_ref, f32[4,4,2,2,32,256]{5,4,3,2,1,0:T(8,128)} %all-to-all-done.refs_0_, f32[66,8,2,128,128]{4,3,2,1,0:T(8,128)} %shard_map.39.refs_1_), custom_call_target="tpu_custom_call", output_to_operand_aliasing={{}: (2, {})} | custom-call | flops 2013265920 | bytes 4718592 | tf_op jit(solution)/shard_map/pallas_call | solution.py:127
  280.4 14.3 %shard_map.41.refs_2_ = f32[66,8,2,128,128]{4,3,2,1,0:T(8,128)} custom-call(s32[132]{0:T(256)S(1)} %reshape.62.slots_ref, f32[4,4,2,2,32,256]{5,4,3,2,1,0:T(8,128)S(1)} %all_to_all.25.refs_0_, f32[4,4,2,2,32,256]{5,4,3,2,1,0:T(8,128)} %collective-permute-done.12.refs_1_, f32[66,8,2,128,128]{4,3,2,1,0:T(8,128)} %shard_map.40.refs_2_), custom_call_target="tpu_custom_call", output_to_operand_aliasing={{}: (3, {})} | custom-call | flops 3221225472 | bytes 8388608 | tf_op jit(solution)/shard_map/pallas_call | solution.py:127
  294.7 14.3 %shard_map.42.refs_2_ = f32[66,8,2,128,128]{4,3,2,1,0:T(8,128)} custom-call(s32[132]{0:T(256)S(1)} %reshape.62.slots_ref, f32[4,4,2,2,32,256]{5,4,3,2,1,0:T(8,128)S(1)} %copy-done.1, f32[4,4,2,2,32,256]{5,4,3,2,1,0:T(8,128)} %collective-permute-done.8.refs_1_, f32[66,8,2,128,128]{4,3,2,1,0:T(8,128)} %shard_map.41.refs_2_), custom_call_target="tpu_custom_call", output_to_operand_aliasing={{}: (3, {})} | custom-call | flops 3221225472 | bytes 8388608 | tf_op jit(solution)/shard_map/pallas_call | solution.py:127
  309.0 14.6 %shard_map.43.refs_2_ = f32[66,8,2,128,128]{4,3,2,1,0:T(8,128)} custom-call(s32[132]{0:T(256)S(1)} %reshape.62.slots_ref, f32[4,4,2,2,32,256]{5,4,3,2,1,0:T(8,128)} %all-to-all-done.2.refs_0_, f32[4,4,2,2,32,256]{5,4,3,2,1,0:T(8,128)} %collective-permute-done.4.refs_1_, f32[66,8,2,128,128]{4,3,2,1,0:T(8,128)} %shard_map.42.refs_2_), custom_call_target="tpu_custom_call", output_to_operand_aliasing={{}: (3, {})} | custom-call | flops 3221225472 | bytes 8388608 | tf_op jit(solution)/shard_map/pallas_call | solution.py:127
  323.6 14.6 %shard_map.44.refs_2_ = f32[66,8,2,128,128]{4,3,2,1,0:T(8,128)} custom-call(s32[132]{0:T(256)S(1)} %reshape.62.slots_ref, f32[4,4,2,2,32,256]{5,4,3,2,1,0:T(8,128)} %all-to-all-done.refs_0_, f32[4,4,2,2,32,256]{5,4,3,2,1,0:T(8,128)} %all-to-all-done.1.refs_1_, f32[66,8,2,128,128]{4,3,2,1,0:T(8,128)} %shard_map.43.refs_2_), custom_call_target="tpu_custom_call", output_to_operand_aliasing={{}: (3, {})} | custom-call | flops 3221225472 | bytes 8388608 | tf_op jit(solution)/shard_map/pallas_call | solution.py:127
  338.2 14.3 %shard_map.45.refs_2_ = f32[66,8,2,128,128]{4,3,2,1,0:T(8,128)} custom-call(s32[132]{0:T(256)S(1)} %reshape.62.slots_ref, f32[4,4,2,2,32,256]{5,4,3,2,1,0:T(8,128)S(1)} %all_to_all.25.refs_0_, f32[4,4,2,2,32,256]{5,4,3,2,1,0:T(8,128)} %collective-permute-done.13.refs_1_, f32[66,8,2,128,128]{4,3,2,1,0:T(8,128)} %shard_map.44.refs_2_), custom_call_target="tpu_custom_call", output_to_operand_aliasing={{}: (3, {})} | custom-call | flops 3221225472 | bytes 8388608 | tf_op jit(solution)/shard_map/pallas_call | solution.py:127
  352.5 0.0 collective-permute-done.14.refs_1_
  352.6 0.1 collective-permute-start.15
  352.6 0.0 collective-permute-done.10.refs_1_
  352.6 1.8 collective-permute-start.11
  354.5 14.3 %shard_map.46.refs_2_ = f32[66,8,2,128,128]{4,3,2,1,0:T(8,128)} custom-call(s32[132]{0:T(256)S(1)} %reshape.62.slots_ref, f32[4,4,2,2,32,256]{5,4,3,2,1,0:T(8,128)S(1)} %copy-done.1, f32[4,4,2,2,32,256]{5,4,3,2,1,0:T(8,128)} %collective-permute-done.9.refs_1_, f32[66,8,2,128,128]{4,3,2,1,0:T(8,128)} %shard_map.45.refs_2_), custom_call_target="tpu_custom_call", output_to_operand_aliasing={{}: (3, {})} | custom-call | flops 3221225472 | bytes 8388608 | tf_op jit(solution)/shard_map/pallas_call | solution.py:127
  368.8 0.3 collective-permute-start.7
  369.1 0.0 collective-permute-done.2.refs_1_
  369.1 0.5 collective-permute-start.3
  369.6 14.6 %shard_map.47.refs_2_ = f32[66,8,2,128,128]{4,3,2,1,0:T(8,128)} custom-call(s32[132]{0:T(256)S(1)} %reshape.62.slots_ref, f32[4,4,2,2,32,256]{5,4,3,2,1,0:T(8,128)} %all-to-all-done.2.refs_0_, f32[4,4,2,2,32,256]{5,4,3,2,1,0:T(8,128)} %collective-permute-done.5.refs_1_, f32[66,8,2,128,128]{4,3,2,1,0:T(8,128)} %shard_map.46.refs_2_), custom_call_target="tpu_custom_call", output_to_operand_aliasing={{}: (3, {})} | custom-call | flops 3221225472 | bytes 8388608 | tf_op jit(solution)/shard_map/pallas_call | solution.py:127
  384.2 14.6 %shard_map.48.refs_2_ = f32[66,8,2,128,128]{4,3,2,1,0:T(8,128)} custom-call(s32[132]{0:T(256)S(1)} %reshape.62.slots_ref, f32[4,4,2,2,32,256]{5,4,3,2,1,0:T(8,128)} %all-to-all-done.refs_0_, f32[4,4,2,2,32,256]{5,4,3,2,1,0:T(8,128)} %collective-permute-done.1.refs_1_, f32[66,8,2,128,128]{4,3,2,1,0:T(8,128)} %shard_map.47.refs_2_), custom_call_target="tpu_custom_call", output_to_operand_aliasing={{}: (3, {})} | custom-call | flops 3221225472 | bytes 8388608 | tf_op jit(solution)/shard_map/pallas_call | solution.py:127
  398.8 14.3 %shard_map.49.refs_2_ = f32[66,8,2,128,128]{4,3,2,1,0:T(8,128)} custom-call(s32[132]{0:T(256)S(1)} %reshape.62.slots_ref, f32[4,4,2,2,32,256]{5,4,3,2,1,0:T(8,128)S(1)} %all_to_all.25.refs_0_, f32[4,4,2,2,32,256]{5,4,3,2,1,0:T(8,128)} %collective-permute-done.14.refs_1_, f32[66,8,2,128,128]{4,3,2,1,0:T(8,128)} %shard_map.48.refs_2_), custom_call_target="tpu_custom_call", output_to_operand_aliasing={{}: (3, {})} | custom-call | flops 3221225472 | bytes 8388608 | tf_op jit(solution)/shard_map/pallas_call | solution.py:127
  413.1 14.3 %shard_map.50.refs_2_ = f32[66,8,2,128,128]{4,3,2,1,0:T(8,128)} custom-call(s32[132]{0:T(256)S(1)} %reshape.62.slots_ref, f32[4,4,2,2,32,256]{5,4,3,2,1,0:T(8,128)S(1)} %copy-done.1, f32[4,4,2,2,32,256]{5,4,3,2,1,0:T(8,128)} %collective-permute-done.10.refs_1_, f32[66,8,2,128,128]{4,3,2,1,0:T(8,128)} %shard_map.49.refs_2_), custom_call_target="tpu_custom_call", output_to_operand_aliasing={{}: (3, {})} | custom-call | flops 3221225472 | bytes 8388608 | tf_op jit(solution)/shard_map/pallas_call | solution.py:127
  427.4 14.6 %shard_map.51.refs_2_ = f32[66,8,2,128,128]{4,3,2,1,0:T(8,128)} custom-call(s32[132]{0:T(256)S(1)} %reshape.62.slots_ref, f32[4,4,2,2,32,256]{5,4,3,2,1,0:T(8,128)} %all-to-all-done.2.refs_0_, f32[4,4,2,2,32,256]{5,4,3,2,1,0:T(8,128)} %collective-permute-done.6.refs_1_, f32[66,8,2,128,128]{4,3,2,1,0:T(8,128)} %shard_map.50.refs_2_), custom_call_target="tpu_custom_call", output_to_operand_aliasing={{}: (3, {})} | custom-call | flops 3221225472 | bytes 8388608 | tf_op jit(solution)/shard_map/pallas_call | solution.py:127
  442.0 14.6 %shard_map.52.refs_2_ = f32[66,8,2,128,128]{4,3,2,1,0:T(8,128)} custom-call(s32[132]{0:T(256)S(1)} %reshape.62.slots_ref, f32[4,4,2,2,32,256]{5,4,3,2,1,0:T(8,128)} %all-to-all-done.refs_0_, f32[4,4,2,2,32,256]{5,4,3,2,1,0:T(8,128)} %collective-permute-done.2.refs_1_, f32[66,8,2,128,128]{4,3,2,1,0:T(8,128)} %shard_map.51.refs_2_), custom_call_target="tpu_custom_call", output_to_operand_aliasing={{}: (3, {})} | custom-call | flops 3221225472 | bytes 8388608 | tf_op jit(solution)/shard_map/pallas_call | solution.py:127
  456.6 0.0 collective-permute-done.15.refs_1_
  456.6 8.9 %shard_map.53.refs_2_ = f32[66,8,2,128,128]{4,3,2,1,0:T(8,128)} custom-call(s32[132]{0:T(256)S(1)} %reshape.62.slots_ref, f32[4,4,2,2,32,256]{5,4,3,2,1,0:T(8,128)S(1)} %all_to_all.25.refs_0_, f32[4,4,2,2,32,256]{5,4,3,2,1,0:T(8,128)} %collective-permute-done.15.refs_1_, f32[66,8,2,128,128]{4,3,2,1,0:T(8,128)} %shard_map.52.refs_2_), custom_call_target="tpu_custom_call", output_to_operand_aliasing={{}: (3, {})} | custom-call | flops 1610612736 | bytes 6291456 | tf_op jit(solution)/shard_map/pallas_call | solution.py:127
  465.5 0.0 collective-permute-done.11.refs_1_
  465.5 8.9 %shard_map.54.refs_2_ = f32[66,8,2,128,128]{4,3,2,1,0:T(8,128)} custom-call(s32[132]{0:T(256)S(1)} %reshape.62.slots_ref, f32[4,4,2,2,32,256]{5,4,3,2,1,0:T(8,128)S(1)} %copy-done.1, f32[4,4,2,2,32,256]{5,4,3,2,1,0:T(8,128)} %collective-permute-done.11.refs_1_, f32[66,8,2,128,128]{4,3,2,1,0:T(8,128)} %shard_map.53.refs_2_), custom_call_target="tpu_custom_call", output_to_operand_aliasing={{}: (3, {})} | custom-call | flops 1610612736 | bytes 6291456 | tf_op jit(solution)/shard_map/pallas_call | solution.py:127
  474.4 9.1 %shard_map.55.refs_2_ = f32[66,8,2,128,128]{4,3,2,1,0:T(8,128)} custom-call(s32[132]{0:T(256)S(1)} %reshape.62.slots_ref, f32[4,4,2,2,32,256]{5,4,3,2,1,0:T(8,128)} %all-to-all-done.2.refs_0_, f32[4,4,2,2,32,256]{5,4,3,2,1,0:T(8,128)} %collective-permute-done.7.refs_1_, f32[66,8,2,128,128]{4,3,2,1,0:T(8,128)} %shard_map.54.refs_2_), custom_call_target="tpu_custom_call", output_to_operand_aliasing={{}: (3, {})} | custom-call | flops 1610612736 | bytes 6291456 | tf_op jit(solution)/shard_map/pallas_call | solution.py:127
  483.5 0.0 collective-permute-done.3.refs_1_
  483.5 9.1 %shard_map.56 = f32[66,8,2,128,128]{4,3,2,1,0:T(8,128)} custom-call(s32[132]{0:T(256)S(1)} %reshape.62.slots_ref, f32[4,4,2,2,32,256]{5,4,3,2,1,0:T(8,128)} %all-to-all-done.refs_0_, f32[4,4,2,2,32,256]{5,4,3,2,1,0:T(8,128)} %collective-permute-done.3.refs_1_, f32[66,8,2,128,128]{4,3,2,1,0:T(8,128)} %shard_map.55.refs_2_), custom_call_target="tpu_custom_call", output_to_operand_aliasing={{}: (3, {})} | custom-call | flops 1610612736 | bytes 6291456 | tf_op jit(solution)/shard_map/pallas_call | solution.py:127
  (14 shorter events, 0.1 us)
Async XLA Ops:
  0.0 7.0 %copy-start.3 = (s32[64]{0:T(128)S(1)}, s32[64]{0:T(128)}, u32[]{:S(2)}) copy-start(s32[64]{0:T(128)} %param.5) | copy-start | bytes 772
  71.3 26.7 %all-to-all-start.2 = ((f32[4,4,2,2,32,256]{5,4,3,2,1,0:T(8,128)}), f32[4,4,2,2,32,256]{5,4,3,2,1,0:T(8,128)}, u32[]{:S(2)}, u32[]{:S(2)}) async-start(f32[4,4,2,2,32,256]{5,4,3,2,1,0:T(8,128)} %get-tuple-element.10), calls=%async_computation.2 | async-start | bytes 4194304 | tf_op jit(solution)/shard_map/all_to_all | solution.py:18
  75.8 24.5 %collective-permute-start = (f32[4,4,2,2,32,256]{5,4,3,2,1,0:T(8,128)}, f32[4,4,2,2,32,256]{5,4,3,2,1,0:T(8,128)}, u32[]{:S(2)}, u32[]{:S(2)}) collective-permute-start(f32[4,4,2,2,32,256]{5,4,3,2,1,0:T(8,128)} %get-tuple-element.12), channel_id=1, source_target_pairs={{0,7},{1,0},{2,1},{3,2},{4,3},{5,4},{6,5},{7,6},{8,15},{9,8},{10,9... | collective-permute-start | bytes 6291464 | tf_op jit(solution)/shard_map/ppermute | solution.py:14
  75.9 46.2 %collective-permute-start.12 = (f32[4,4,2,2,32,256]{5,4,3,2,1,0:T(8,128)S(1)}, f32[4,4,2,2,32,256]{5,4,3,2,1,0:T(8,128)}, u32[]{:S(2)}, u32[]{:S(2)}) collective-permute-start(f32[4,4,2,2,32,256]{5,4,3,2,1,0:T(8,128)S(1)} %all_to_all.25.refs_0_), channel_id=1, source_target_pairs={{0,7},{1,0},{2,1},{3,2},{4,3},{5,4},{6,5},{7,6},{8,15},{9,8},{10,9... | collective-permute-start | bytes 6291464 | tf_op jit(solution)/shard_map/ppermute | solution.py:14
  79.6 65.2 %collective-permute-start.8 = (f32[4,4,2,2,32,256]{5,4,3,2,1,0:T(8,128)}, f32[4,4,2,2,32,256]{5,4,3,2,1,0:T(8,128)}, u32[]{:S(2)}, u32[]{:S(2)}) collective-permute-start(f32[4,4,2,2,32,256]{5,4,3,2,1,0:T(8,128)} %all_to_all.26.refs_0_), channel_id=1, source_target_pairs={{0,7},{1,0},{2,1},{3,2},{4,3},{5,4},{6,5},{7,6},{8,15},{9,8},{10,9... | collective-permute-start | bytes 6291464 | tf_op jit(solution)/shard_map/ppermute | solution.py:14
  98.0 69.2 %collective-permute-start.4 = (f32[4,4,2,2,32,256]{5,4,3,2,1,0:T(8,128)}, f32[4,4,2,2,32,256]{5,4,3,2,1,0:T(8,128)}, u32[]{:S(2)}, u32[]{:S(2)}) collective-permute-start(f32[4,4,2,2,32,256]{5,4,3,2,1,0:T(8,128)} %all-to-all-done.2.refs_0_), channel_id=1, source_target_pairs={{0,7},{1,0},{2,1},{3,2},{4,3},{5,4},{6,5},{7,6},{8,15},{9,8},{10,9... | collective-permute-start | bytes 6291464 | tf_op jit(solution)/shard_map/ppermute | solution.py:14
  100.3 70.7 %all-to-all-start.1 = ((f32[4,4,2,2,32,256]{5,4,3,2,1,0:T(8,128)}), f32[4,4,2,2,32,256]{5,4,3,2,1,0:T(8,128)}, u32[]{:S(2)}, u32[]{:S(2)}) async-start(f32[4,4,2,2,32,256]{5,4,3,2,1,0:T(8,128)} %collective-permute-done), calls=%async_computation.1 | async-start | bytes 4194304 | tf_op jit(solution)/shard_map/all_to_all | solution.py:18
  104.8 70.6 %copy-start.2 = (s32[66,2]{0,1:T(2,128)S(1)}, s32[66,2]{0,1:T(2,128)}, u32[]{:S(2)}) copy-start(s32[66,2]{0,1:T(2,128)} %param.4) | copy-start | bytes 1588
  122.2 67.5 %collective-permute-start.13 = (f32[4,4,2,2,32,256]{5,4,3,2,1,0:T(8,128)}, f32[4,4,2,2,32,256]{5,4,3,2,1,0:T(8,128)}, u32[]{:S(2)}, u32[]{:S(2)}) collective-permute-start(f32[4,4,2,2,32,256]{5,4,3,2,1,0:T(8,128)} %collective-permute-done.12.refs_1_), channel_id=1, source_target_pairs={{0,7},{1,0},{2,1},{3,2},{4,3},{5,4},{6,5},{7,6},{8,15},{9,8},{10,9... | collective-permute-start | bytes 6291464 | tf_op jit(solution)/shard_map/ppermute | solution.py:14
  144.7 67.4 %collective-permute-start.9 = (f32[4,4,2,2,32,256]{5,4,3,2,1,0:T(8,128)}, f32[4,4,2,2,32,256]{5,4,3,2,1,0:T(8,128)}, u32[]{:S(2)}, u32[]{:S(2)}) collective-permute-start(f32[4,4,2,2,32,256]{5,4,3,2,1,0:T(8,128)} %collective-permute-done.8.refs_1_), channel_id=1, source_target_pairs={{0,7},{1,0},{2,1},{3,2},{4,3},{5,4},{6,5},{7,6},{8,15},{9,8},{10,9... | collective-permute-start | bytes 6291464 | tf_op jit(solution)/shard_map/ppermute | solution.py:14
  167.2 67.4 %collective-permute-start.5 = (f32[4,4,2,2,32,256]{5,4,3,2,1,0:T(8,128)}, f32[4,4,2,2,32,256]{5,4,3,2,1,0:T(8,128)}, u32[]{:S(2)}, u32[]{:S(2)}) collective-permute-start(f32[4,4,2,2,32,256]{5,4,3,2,1,0:T(8,128)} %collective-permute-done.4.refs_1_), channel_id=1, source_target_pairs={{0,7},{1,0},{2,1},{3,2},{4,3},{5,4},{6,5},{7,6},{8,15},{9,8},{10,9... | collective-permute-start | bytes 6291464 | tf_op jit(solution)/shard_map/ppermute | solution.py:14
  170.9 86.2 %collective-permute-start.1 = (f32[4,4,2,2,32,256]{5,4,3,2,1,0:T(8,128)}, f32[4,4,2,2,32,256]{5,4,3,2,1,0:T(8,128)}, u32[]{:S(2)}, u32[]{:S(2)}) collective-permute-start(f32[4,4,2,2,32,256]{5,4,3,2,1,0:T(8,128)} %all-to-all-done.1.refs_1_), channel_id=1, source_target_pairs={{0,7},{1,0},{2,1},{3,2},{4,3},{5,4},{6,5},{7,6},{8,15},{9,8},{10,9... | collective-permute-start | bytes 6291464 | tf_op jit(solution)/shard_map/ppermute | solution.py:14
  171.0 99.6 %all-to-all-start = ((f32[4,4,2,2,32,256]{5,4,3,2,1,0:T(8,128)}), f32[4,4,2,2,32,256]{5,4,3,2,1,0:T(8,128)}, u32[]{:S(2)}, u32[]{:S(2)}) async-start(f32[4,4,2,2,32,256]{5,4,3,2,1,0:T(8,128)} %get-tuple-element.12), calls=%async_computation | async-start | bytes 4194304 | tf_op jit(solution)/shard_map/all_to_all | solution.py:18
  175.7 48.9 %copy-start = (f32[4,4,2,2,32,256]{5,4,3,2,1,0:T(8,128)S(1)}, f32[4,4,2,2,32,256]{5,4,3,2,1,0:T(8,128)}, u32[]{:S(2)}) copy-start(f32[4,4,2,2,32,256]{5,4,3,2,1,0:T(8,128)} %all_to_all.26.refs_0_) | copy-start | bytes 6291460
  189.7 162.9 %collective-permute-start.14 = (f32[4,4,2,2,32,256]{5,4,3,2,1,0:T(8,128)}, f32[4,4,2,2,32,256]{5,4,3,2,1,0:T(8,128)}, u32[]{:S(2)}, u32[]{:S(2)}) collective-permute-start(f32[4,4,2,2,32,256]{5,4,3,2,1,0:T(8,128)} %collective-permute-done.13.refs_1_), channel_id=1, source_target_pairs={{0,7},{1,0},{2,1},{3,2},{4,3},{5,4},{6,5},{7,6},{8,15},{9,8},{10,9... | collective-permute-start | bytes 6291464 | tf_op jit(solution)/shard_map/ppermute | solution.py:14
  212.2 140.5 %collective-permute-start.10 = (f32[4,4,2,2,32,256]{5,4,3,2,1,0:T(8,128)}, f32[4,4,2,2,32,256]{5,4,3,2,1,0:T(8,128)}, u32[]{:S(2)}, u32[]{:S(2)}) collective-permute-start(f32[4,4,2,2,32,256]{5,4,3,2,1,0:T(8,128)} %collective-permute-done.9.refs_1_), channel_id=1, source_target_pairs={{0,7},{1,0},{2,1},{3,2},{4,3},{5,4},{6,5},{7,6},{8,15},{9,8},{10,9... | collective-permute-start | bytes 6291464 | tf_op jit(solution)/shard_map/ppermute | solution.py:14
  234.6 134.2 %collective-permute-start.6 = (f32[4,4,2,2,32,256]{5,4,3,2,1,0:T(8,128)}, f32[4,4,2,2,32,256]{5,4,3,2,1,0:T(8,128)}, u32[]{:S(2)}, u32[]{:S(2)}) collective-permute-start(f32[4,4,2,2,32,256]{5,4,3,2,1,0:T(8,128)} %collective-permute-done.5.refs_1_), channel_id=1, source_target_pairs={{0,7},{1,0},{2,1},{3,2},{4,3},{5,4},{6,5},{7,6},{8,15},{9,8},{10,9... | collective-permute-start | bytes 6291464 | tf_op jit(solution)/shard_map/ppermute | solution.py:14
  257.1 112.0 %collective-permute-start.2 = (f32[4,4,2,2,32,256]{5,4,3,2,1,0:T(8,128)}, f32[4,4,2,2,32,256]{5,4,3,2,1,0:T(8,128)}, u32[]{:S(2)}, u32[]{:S(2)}) collective-permute-start(f32[4,4,2,2,32,256]{5,4,3,2,1,0:T(8,128)} %collective-permute-done.1.refs_1_), channel_id=1, source_target_pairs={{0,7},{1,0},{2,1},{3,2},{4,3},{5,4},{6,5},{7,6},{8,15},{9,8},{10,9... | collective-permute-start | bytes 6291464 | tf_op jit(solution)/shard_map/ppermute | solution.py:14
  280.3 14.3 %copy-start.1 = (f32[4,4,2,2,32,256]{5,4,3,2,1,0:T(8,128)S(1)}, f32[4,4,2,2,32,256]{5,4,3,2,1,0:T(8,128)}, u32[]{:S(2)}) copy-start(f32[4,4,2,2,32,256]{5,4,3,2,1,0:T(8,128)} %all_to_all.26.refs_0_) | copy-start | bytes 6291460
  352.6 104.1 %collective-permute-start.15 = (f32[4,4,2,2,32,256]{5,4,3,2,1,0:T(8,128)}, f32[4,4,2,2,32,256]{5,4,3,2,1,0:T(8,128)}, u32[]{:S(2)}, u32[]{:S(2)}) collective-permute-start(f32[4,4,2,2,32,256]{5,4,3,2,1,0:T(8,128)} %collective-permute-done.14.refs_1_), channel_id=1, source_target_pairs={{0,7},{1,0},{2,1},{3,2},{4,3},{5,4},{6,5},{7,6},{8,15},{9,8},{10,9... | collective-permute-start | bytes 6291464 | tf_op jit(solution)/shard_map/ppermute | solution.py:14
  352.6 112.9 %collective-permute-start.11 = (f32[4,4,2,2,32,256]{5,4,3,2,1,0:T(8,128)}, f32[4,4,2,2,32,256]{5,4,3,2,1,0:T(8,128)}, u32[]{:S(2)}, u32[]{:S(2)}) collective-permute-start(f32[4,4,2,2,32,256]{5,4,3,2,1,0:T(8,128)} %collective-permute-done.10.refs_1_), channel_id=1, source_target_pairs={{0,7},{1,0},{2,1},{3,2},{4,3},{5,4},{6,5},{7,6},{8,15},{9,8},{10,9... | collective-permute-start | bytes 6291464 | tf_op jit(solution)/shard_map/ppermute | solution.py:14
  368.8 105.6 %collective-permute-start.7 = (f32[4,4,2,2,32,256]{5,4,3,2,1,0:T(8,128)}, f32[4,4,2,2,32,256]{5,4,3,2,1,0:T(8,128)}, u32[]{:S(2)}, u32[]{:S(2)}) collective-permute-start(f32[4,4,2,2,32,256]{5,4,3,2,1,0:T(8,128)} %collective-permute-done.6.refs_1_), channel_id=1, source_target_pairs={{0,7},{1,0},{2,1},{3,2},{4,3},{5,4},{6,5},{7,6},{8,15},{9,8},{10,9... | collective-permute-start | bytes 6291464 | tf_op jit(solution)/shard_map/ppermute | solution.py:14
  369.1 114.4 %collective-permute-start.3 = (f32[4,4,2,2,32,256]{5,4,3,2,1,0:T(8,128)}, f32[4,4,2,2,32,256]{5,4,3,2,1,0:T(8,128)}, u32[]{:S(2)}, u32[]{:S(2)}) collective-permute-start(f32[4,4,2,2,32,256]{5,4,3,2,1,0:T(8,128)} %collective-permute-done.2.refs_1_), channel_id=1, source_target_pairs={{0,7},{1,0},{2,1},{3,2},{4,3},{5,4},{6,5},{7,6},{8,15},{9,8},{10,9... | collective-permute-start | bytes 6291464 | tf_op jit(solution)/shard_map/ppermute | solution.py:14

commit v2 on v1

v2 whole, which is shorter than its diff:
```python
import functools

import jax
import jax.numpy as jnp
from jax import lax
from jax.experimental import pallas as pl
from jax.experimental.pallas import tpu as pltpu
from jax.sharding import PartitionSpec as P


def passed_along(value, axis):
    count = lax.axis_size(axis)
    pairs = [(source, (source - 1) % count) for source in range(count)]
    return lax.ppermute(value, axis, pairs)


def turn_kernel(chunks, volts, *refs):
    own = refs[:chunks]
    far = refs[chunks : 2 * chunks - 1]
    local_sem, send_sem, recv_sem, pass_send, pass_recv = refs[2 * chunks - 1 :]
    count = lax.axis_size("freq")
    me = lax.axis_index("freq")
    blk_count = lax.axis_size("blk")
    here = lax.axis_index("blk")
    before = lax.rem(here + blk_count - 1, blk_count)
    after = lax.rem(here + 1, blk_count)
    chan_dev = volts.shape[1] // count
    per_chunk = chan_dev // chunks

    barrier = pltpu.get_barrier_semaphore()
    for shift in range(1, count):
        pl.semaphore_signal(
            barrier,
            inc=1,
            device_id=(lax.rem(me + shift, count), here),
            device_id_type=pl.DeviceIdType.MESH,
        )
    for other in (before, after):
        pl.semaphore_signal(
            barrier, inc=1, device_id=(me, other), device_id_type=pl.DeviceIdType.MESH
        )
    pl.semaphore_wait(barrier, count + 1)

    def part(device, g):
        return volts.at[:, pl.ds(device * chan_dev + g * per_chunk, per_chunk)]

    kept, sent, passed = [], [], []
    for g in range(chunks):
        kept.append(pltpu.make_async_copy(part(me, g), own[g].at[me], local_sem.at[g]))
        kept[g].start()
        sent.append([])
        for shift in range(1, count):
            peer = lax.rem(me + shift, count)
            copy = pltpu.make_async_remote_copy(
                src_ref=part(peer, g),
                dst_ref=own[g].at[me],
                send_sem=send_sem.at[g, shift - 1],
                recv_sem=recv_sem.at[g, shift - 1],
                device_id=(peer, here),
                device_id_type=pl.DeviceIdType.MESH,
            )
            copy.start()
            sent[g].append(copy)
    for g in range(chunks):
        kept[g].wait()
        for copy in sent[g]:
            copy.wait_recv()
        if g < chunks - 1:
            copy = pltpu.make_async_remote_copy(
                src_ref=own[g],
                dst_ref=far[g],
                send_sem=pass_send.at[g],
                recv_sem=pass_recv.at[g],
                device_id=(me, before),
                device_id_type=pl.DeviceIdType.MESH,
            )
            copy.start()
            passed.append(copy)
    for g in range(chunks):
        for copy in sent[g]:
            copy.wait_send()
    for copy in passed:
        copy.wait()


def turned(voltages, chunks):
    count = lax.axis_size("freq")
    per_dev, chans, _, rows, samples = voltages.shape
    per_chunk = chans // count // chunks
    piece = jax.ShapeDtypeStruct(
        (count, per_dev, per_chunk, 2, rows, samples), voltages.dtype
    )
    any_spec = pl.BlockSpec(memory_space=pl.ANY)
    made = 2 * chunks - 1
    outs = pl.pallas_call(
        functools.partial(turn_kernel, chunks),
        out_shape=[piece] * made,
        in_specs=[any_spec],
        out_specs=[any_spec] * made,
        scratch_shapes=[
            pltpu.SemaphoreType.DMA((chunks,)),
            pltpu.SemaphoreType.DMA((chunks, count - 1)),
            pltpu.SemaphoreType.DMA((chunks, count - 1)),
            pltpu.SemaphoreType.DMA((chunks,)),
            pltpu.SemaphoreType.DMA((chunks,)),
        ],
        compiler_params=pltpu.CompilerParams(collective_id=0, has_side_effects=True),
        cost_estimate=pl.CostEstimate(
            flops=0, bytes_accessed=8 * voltages.size, transcendentals=0
        ),
    )(voltages)
    return list(outs[:chunks]), list(outs[chunks:])


def tiles_kernel(start, count, chan0, steps, n_sets, has_prev, slots_ref, *refs):
    sets = refs[:n_sets]
    keep_ref = refs[n_sets]
    out_ref, left, right_hi, right_lo, stage, sems = refs[n_sets + 1 + has_prev :]
    step = pl.program_id(0)
    slot = lax.rem(step, 2)
    groups, per_dev, _, rows, samples = sets[0].shape
    width = groups * rows
    scale = 1.0 / samples

    def copy_out(which, channel):
        return pltpu.make_async_copy(
            stage.at[which],
            out_ref.at[pl.ds(start, count), chan0 + channel],
            sems.at[which],
        )

    def halves(value):
        head = value.astype(jnp.bfloat16)
        return head, (value - head.astype(jnp.float32)).astype(jnp.bfloat16)

    for index, ref in enumerate(sets):
        for block in range(per_dev):
            at = index * per_dev + block
            keep = keep_ref[at]
            re = ref[:, block, 0].reshape(width, samples) * keep
            im = ref[:, block, 1].reshape(width, samples) * keep
            for column, value in ((0, re), (samples, im)):
                head, tail = halves(value)
                left[at, :width, column : column + samples] = head
                left[at, width:, column : column + samples] = tail
            re = re.T
            im = im.T
            for row, column, value in (
                (0, 0, re),
                (samples, 0, im),
                (0, width, -im),
                (samples, width, re),
            ):
                head, tail = halves(value)
                right_hi[at, row : row + samples, column : column + width] = head
                right_lo[at, row : row + samples, column : column + width] = tail

    if steps > 2:

        @pl.when(step >= 2)
        def _():
            copy_out(slot, step - 2).wait()

    def dot(a, b):
        return jnp.dot(a, b, preferred_element_type=jnp.float32)

    def tile(index, carry):
        x = slots_ref[2 * (start + index)]
        y = slots_ref[2 * (start + index) + 1]
        by_head = dot(left[x], right_hi[y])
        by_tail = dot(left[x, :width, :], right_lo[y])
        total = (by_head[width:] + by_tail + by_head[:width]) * scale
        stage[slot, index, 0] = total[:, :width]
        stage[slot, index, 1] = total[:, width:]
        return carry

    lax.fori_loop(0, count, tile, 0, unroll=2 if count % 2 == 0 else 1)
    copy_out(slot, step).start()

    @pl.when(step == steps - 1)
    def _():
        if steps > 1:
            copy_out(lax.rem(step + 1, 2), step - 1).wait()
        copy_out(slot, step).wait()


def place_group(prev, out_type, slots, start, count, chan0, sets, keep):
    groups, per_dev, steps, _, rows, samples = sets[0].shape
    width = groups * rows
    n_sets = len(sets)
    has_prev = 0 if prev is None else 1
    spec = pl.BlockSpec(
        (groups, per_dev, None, 2, rows, samples), lambda c, *_: (0, 0, c, 0, 0, 0)
    )
    any_spec = pl.BlockSpec(memory_space=pl.ANY)
    flops = 3 * 3 * 2 * 2 * width * width * 2 * samples * count * steps
    moved = 4 * (sum(one.size for one in sets) + 2 * width * width * count * steps)
    call = pl.pallas_call(
        functools.partial(tiles_kernel, start, count, chan0, steps, n_sets, has_prev),
        out_shape=out_type,
        grid_spec=pltpu.PrefetchScalarGridSpec(
            num_scalar_prefetch=1,
            grid=(steps,),
            in_specs=[spec] * n_sets
            + [pl.BlockSpec(keep.shape, lambda c, *_: (0, 0, 0))]
            + [any_spec] * has_prev,
            out_specs=any_spec,
            scratch_shapes=[
                pltpu.VMEM((n_sets * per_dev, 2 * width, 2 * samples), jnp.bfloat16),
                pltpu.VMEM((n_sets * per_dev, 2 * samples, 2 * width), jnp.bfloat16),
                pltpu.VMEM((n_sets * per_dev, 2 * samples, 2 * width), jnp.bfloat16),
                pltpu.VMEM((2, count, 2, width, width), jnp.float32),
                pltpu.SemaphoreType.DMA((2,)),
            ],
        ),
        input_output_aliases={2 + n_sets: 0} if has_prev else {},
        compiler_params=pltpu.CompilerParams(
            dimension_semantics=("arbitrary",), vmem_limit_bytes=32 * 1024 * 1024
        ),
        cost_estimate=pl.CostEstimate(
            flops=flops, bytes_accessed=moved, transcendentals=0
        ),
    )
    return call(slots, *sets, keep, *([prev] if has_prev else []))


def shards(voltages, pair_table, bad_feeds):
    blk_count = lax.axis_size("blk")
    freq_count = lax.axis_size("freq")
    here = lax.axis_index("blk")
    per_dev, chans, _, rows, samples = voltages.shape
    width = rows * freq_count
    chan_dev = chans // freq_count
    half = blk_count // 2
    chunks = 4 if per_dev > 1 and chan_dev % 4 == 0 else 1
    per_chunk = chan_dev // chunks
    tile_count = per_dev * per_dev
    own_count = per_dev * (per_dev + 1) // 2
    shared_count = (tile_count + 1) // 2

    def kept(step):
        first = lax.rem(here + step, blk_count) * per_dev * width
        inputs = first + jnp.arange(per_dev * width, dtype=jnp.int32)
        flagged = jnp.any((inputs // 2)[:, None] == bad_feeds[None, :], axis=-1)
        return jnp.where(flagged, 0.0, 1.0).astype(jnp.float32).reshape(per_dev, width, 1)

    slots = jnp.where(
        pair_table // per_dev == here, pair_table % per_dev, per_dev + pair_table % per_dev
    ).reshape(-1)

    own, first_hop = turned(voltages, chunks)
    own_keep = kept(0)

    out_type = jax.ShapeDtypeStruct(
        (pair_table.shape[0], chan_dev, 2, width, width), jnp.float32
    )
    visibility = None
    for g in range(chunks):
        visibility = place_group(
            visibility, out_type, slots, 0, own_count, g * per_chunk, [own[g]], own_keep
        )
    far = own
    for step in range(1, half + 1):
        far = [
            first_hop[g] if step == 1 and g < chunks - 1 else passed_along(far[g], "blk")
            for g in range(chunks)
        ]
        both_keep = jnp.concatenate([own_keep, kept(step)], axis=0)
        for g in range(chunks):
            visibility = place_group(
                visibility,
                out_type,
                slots,
                own_count + (step - 1) * tile_count,
                tile_count if step < half else shared_count,
                g * per_chunk,
                [own[g], far[g]],
                both_keep,
            )
    return visibility


def solution(mesh):
    placed = (P("blk", None, None, "freq", None), P("blk", None), P())
    return jax.shard_map(
        shards,
        mesh=mesh,
        in_specs=placed,
        out_specs=P("blk", "freq", None, None, None),
        check_vma=False,
    )
```

time: 493 us -> 414 us (0.84)
  blocking collectives: 57.7 us -> 0 us
  Pallas kernels: 246 us -> 297 us
  waiting for transfers between devices: 126 us -> 83.6 us
  starting transfers between devices: 48.2 us -> 20.5 us
  other arithmetic: 6.71 us -> 0.27 us
    all_to_all x2 -> x0, blocking collectives: 57.7 us -> none  [turned(): lax.all_to_all(value, 'freq', split_axis=0, concat_axis=0, tiled=True)]
    pallas_call x20 -> x21, Pallas kernels: 246 us -> 297 us  [the longest x20 189 us: place_group(): return call(slots, *sets, keep, *([prev] if has_prev else []))]
    ppermute x16 -> x13, waiting for transfers between devices: 108 us -> 83.6 us  [passed_along(): return lax.ppermute(value, axis, pairs)]
    all_to_all x3 -> x0, waiting for transfers between devices: 18.4 us -> none  [turned(): lax.all_to_all(value, 'freq', split_axis=0, concat_axis=0, tiled=True)]
    ppermute x16 -> x13, starting transfers between devices: 34.8 us -> 20.5 us  [passed_along(): return lax.ppermute(value, axis, pairs)]
    all_to_all x3 -> x0, starting transfers between devices: 13.4 us -> none  [turned(): lax.all_to_all(value, 'freq', split_axis=0, concat_axis=0, tiled=True)]
    unnamed x8 -> x38, local copies, waits for them, and re-layouts: 0.02 us -> 9.04 us
    slice x1 -> x0, local copies, waits for them, and re-layouts: 6.89 us -> none  [shards(): split[:, :, g]]
  transfers between devices with their start and end apart: 19 -> 13, of which waited for: 8 -> 7; matrix products, arithmetic and copies ran while one was open for 0% -> 1% of each run, Pallas kernels for 48% -> 44%
where the time goes in v2:
time: 414 us; the launch traced here: 413 us
  Pallas kernels  297 us (72%)
  waiting for transfers between devices  83.6 us (20%)
  starting transfers between devices  20.5 us (5%)
  local copies, waits for them, and re-layouts  11.1 us (3%)
    pallas_call x20, Pallas kernels, place_group(): return call(slots, *sets, keep, *([prev] if has_prev else []))  189 us
    pallas_call x1, Pallas kernels, turned(): pl.pallas_call(functools.partial(turn_kernel, chunks), out_shape=[piece]...  108 us
    ppermute x13, waiting for transfers between devices, passed_along(): return lax.ppermute(value, axis, pairs)  83.6 us
    ppermute x13, starting transfers between devices, passed_along(): return lax.ppermute(value, axis, pairs)  20.5 us
    unnamed x38, local copies, waits for them, and re-layouts  9.04 us
  transfers between devices with their start and end apart: 13, of which 7 were waited for; matrix products, arithmetic and copies ran while one was open for 1% of the time, Pallas kernels for 44%

profile of v2, /device:TPU:0, one launch (start us, length us, event | category | flops | bytes accessed | tf_op | source)
XLA Modules:
  0.0 413.1 jit_solution(12618350927894229000)
XLA Ops:
  0.0 107.8 %shard_map.37 = (f32[4,4,2,2,32,256]{5,4,3,2,1,0:T(8,128)}, f32[4,4,2,2,32,256]{5,4,3,2,1,0:T(8,128)}, f32[4,4,2,2,32,256]{5,4,3,2,1,0:T(8,128)}, f32[4,4,2,2,32...) custom-call(f32[4,32,2,32,256]{4,3,2,1,0:T(8,128)} %volts.1), custom_call_target="tpu_custom_call" | custom-call | bytes 16777216 | tf_op jit(solution)/shard_map/pallas_call | solution.py:95
  107.8 3.8 collective-permute-start
  111.5 0.1 collective-permute-start.10
  111.6 0.1 collective-permute-start.7
  111.7 0.1 collective-permute-start.4
  111.8 0.0 copy-done.18
  111.8 0.2 compare_reduce_fusion
  112.0 0.1 copy.61.refs_1_
  112.2 0.0 copy-done.17
  112.2 0.1 copy.57
  112.3 0.1 reshape.169.slots_ref
  112.5 1.6 copy-done.7
  114.1 6.6 %shard_map.38.refs_2_ = f32[66,8,2,128,128]{4,3,2,1,0:T(8,128)} custom-call(s32[132]{0:T(256)S(1)} %reshape.169.slots_ref, f32[4,4,2,2,32,256]{5,4,3,2,1,0:T(8,128)S(1)} %copy-done.7, f32[4,128,1]{2,1,0:T(8,128)S(1)} %copy.61.refs_1_), custom_call_target="tpu_custom_call" | custom-call | flops 6039797760 | bytes 4718592 | tf_op jit(solution)/shard_map/pallas_call | solution.py:224
  120.6 0.0 copy-done.4
  120.7 6.6 %shard_map.39.refs_2_ = f32[66,8,2,128,128]{4,3,2,1,0:T(8,128)} custom-call(s32[132]{0:T(256)S(1)} %reshape.169.slots_ref, f32[4,4,2,2,32,256]{5,4,3,2,1,0:T(8,128)S(1)} %copy-done.4, f32[4,128,1]{2,1,0:T(8,128)S(1)} %copy.61.refs_1_, f32[66,8,2,128,128]{4,3,2,1,0:T(8,128)} %shard_map.38.refs_2_), custom_call_target="tpu_custom_call", output_to_operand_aliasing={{}: (3, {})} | custom-call | flops 6039797760 | bytes 4718592 | tf_op jit(solution)/shard_map/pallas_call | solution.py:224
  127.3 6.6 %shard_map.40.refs_2_ = f32[66,8,2,128,128]{4,3,2,1,0:T(8,128)} custom-call(s32[132]{0:T(256)S(1)} %reshape.169.slots_ref, f32[4,4,2,2,32,256]{5,4,3,2,1,0:T(8,128)S(1)} %copy-done.1, f32[4,128,1]{2,1,0:T(8,128)S(1)} %copy.61.refs_1_, f32[66,8,2,128,128]{4,3,2,1,0:T(8,128)} %shard_map.39.refs_2_), custom_call_target="tpu_custom_call", output_to_operand_aliasing={{}: (3, {})} | custom-call | flops 6039797760 | bytes 4718592 | tf_op jit(solution)/shard_map/pallas_call | solution.py:224
  133.9 6.6 %shard_map.41.refs_3_ = f32[66,8,2,128,128]{4,3,2,1,0:T(8,128)} custom-call(s32[132]{0:T(256)S(1)} %reshape.169.slots_ref, f32[4,4,2,2,32,256]{5,4,3,2,1,0:T(8,128)S(1)} %copy-done, f32[4,128,1]{2,1,0:T(8,128)S(1)} %copy.61.refs_1_, f32[66,8,2,128,128]{4,3,2,1,0:T(8,128)} %shard_map.40.refs_2_), custom_call_target="tpu_custom_call", output_to_operand_aliasing={{}: (3, {})} | custom-call | flops 6039797760 | bytes 4718592 | tf_op jit(solution)/shard_map/pallas_call | solution.py:224
  140.6 0.2 copy.65.refs_2_
  140.8 1.6 copy-done.8
  142.4 1.6 copy-done.16
  144.0 10.1 %shard_map.42.refs_3_ = f32[66,8,2,128,128]{4,3,2,1,0:T(8,128)} custom-call(s32[132]{0:T(256)S(1)} %reshape.169.slots_ref, f32[4,4,2,2,32,256]{5,4,3,2,1,0:T(8,128)S(1)} %copy-done.8, f32[4,4,2,2,32,256]{5,4,3,2,1,0:T(8,128)S(1)} %copy-done.16, f32[8,128,1]{2,1,0:T(8,128)S(1)} %copy.65.refs_2_, ...), custom_call_target="tpu_custom_call", output_to_operand_aliasing={{}: (4, {})} | custom-call | flops 9663676416 | bytes 8388608 | tf_op jit(solution)/shard_map/pallas_call | solution.py:224
  154.2 10.2 %shard_map.43.refs_3_ = f32[66,8,2,128,128]{4,3,2,1,0:T(8,128)} custom-call(s32[132]{0:T(256)S(1)} %reshape.169.slots_ref, f32[4,4,2,2,32,256]{5,4,3,2,1,0:T(8,128)S(1)} %copy-done.5, f32[4,4,2,2,32,256]{5,4,3,2,1,0:T(8,128)S(1)} %copy-done.15, f32[8,128,1]{2,1,0:T(8,128)S(1)} %copy.65.refs_2_, ...), custom_call_target="tpu_custom_call", output_to_operand_aliasing={{}: (4, {})} | custom-call | flops 9663676416 | bytes 8388608 | tf_op jit(solution)/shard_map/pallas_call | solution.py:224
  164.3 1.0 copy.69.refs_2_
  165.4 0.2 copy.73.refs_2_
  165.6 0.2 copy.77.refs_2_
  165.8 1.6 copy-done.2
  167.4 1.0 copy-done.12
  168.5 1.6 copy-done.14
  170.1 10.1 %shard_map.44.refs_3_ = f32[66,8,2,128,128]{4,3,2,1,0:T(8,128)} custom-call(s32[132]{0:T(256)S(1)} %reshape.169.slots_ref, f32[4,4,2,2,32,256]{5,4,3,2,1,0:T(8,128)S(1)} %copy-done.2, f32[4,4,2,2,32,256]{5,4,3,2,1,0:T(8,128)S(1)} %copy-done.14, f32[8,128,1]{2,1,0:T(8,128)S(1)} %copy-done.12, ...), custom_call_target="tpu_custom_call", output_to_operand_aliasing={{}: (4, {})} | custom-call | flops 9663676416 | bytes 8388608 | tf_op jit(solution)/shard_map/pallas_call | solution.py:224
  180.2 0.0 collective-permute-done.refs_1_
  180.2 0.1 collective-permute-start.1
  180.3 11.3 %shard_map.45.refs_3_ = f32[66,8,2,128,128]{4,3,2,1,0:T(8,128)} custom-call(s32[132]{0:T(256)S(1)} %reshape.169.slots_ref, f32[4,4,2,2,32,256]{5,4,3,2,1,0:T(8,128)S(1)} %copy-done, f32[4,4,2,2,32,256]{5,4,3,2,1,0:T(8,128)} %collective-permute-done.refs_1_, f32[8,128,1]{2,1,0:T(8,128)S(1)} %copy-done.13, ...), custom_call_target="tpu_custom_call", output_to_operand_aliasing={{}: (4, {})} | custom-call | flops 9663676416 | bytes 8388608 | tf_op jit(solution)/shard_map/pallas_call | solution.py:224
  191.6 0.0 collective-permute-done.10.refs_1_
  191.6 0.1 collective-permute-start.11
  191.7 0.0 collective-permute-done.7.refs_1_
  191.7 0.3 collective-permute-start.8
  191.9 11.2 %shard_map.46.refs_3_ = f32[66,8,2,128,128]{4,3,2,1,0:T(8,128)} custom-call(s32[132]{0:T(256)S(1)} %reshape.169.slots_ref, f32[4,4,2,2,32,256]{5,4,3,2,1,0:T(8,128)S(1)} %copy-done.9, f32[4,4,2,2,32,256]{5,4,3,2,1,0:T(8,128)} %collective-permute-done.10.refs_1_, f32[8,128,1]{2,1,0:T(8,128)S(1)} %copy-done.10, ...), custom_call_target="tpu_custom_call", output_to_operand_aliasing={{}: (4, {})} | custom-call | flops 9663676416 | bytes 8388608 | tf_op jit(solution)/shard_map/pallas_call | solution.py:224
  203.2 11.2 %shard_map.47.refs_3_ = f32[66,8,2,128,128]{4,3,2,1,0:T(8,128)} custom-call(s32[132]{0:T(256)S(1)} %reshape.169.slots_ref, f32[4,4,2,2,32,256]{5,4,3,2,1,0:T(8,128)S(1)} %copy-done.6, f32[4,4,2,2,32,256]{5,4,3,2,1,0:T(8,128)} %collective-permute-done.7.refs_1_, f32[8,128,1]{2,1,0:T(8,128)S(1)} %copy-done.10, ...), custom_call_target="tpu_custom_call", output_to_operand_aliasing={{}: (4, {})} | custom-call | flops 9663676416 | bytes 8388608 | tf_op jit(solution)/shard_map/pallas_call | solution.py:224
  214.4 0.0 collective-permute-done.4.refs_1_
  214.4 1.2 collective-permute-start.5
  215.6 11.2 %shard_map.48.refs_3_ = f32[66,8,2,128,128]{4,3,2,1,0:T(8,128)} custom-call(s32[132]{0:T(256)S(1)} %reshape.169.slots_ref, f32[4,4,2,2,32,256]{5,4,3,2,1,0:T(8,128)S(1)} %copy-done.3, f32[4,4,2,2,32,256]{5,4,3,2,1,0:T(8,128)} %collective-permute-done.4.refs_1_, f32[8,128,1]{2,1,0:T(8,128)S(1)} %copy-done.10, ...), custom_call_target="tpu_custom_call", output_to_operand_aliasing={{}: (4, {})} | custom-call | flops 9663676416 | bytes 8388608 | tf_op jit(solution)/shard_map/pallas_call | solution.py:224
  226.9 0.0 collective-permute-done.1.refs_1_
  226.9 3.7 collective-permute-start.2
  230.6 11.2 %shard_map.49.refs_3_ = f32[66,8,2,128,128]{4,3,2,1,0:T(8,128)} custom-call(s32[132]{0:T(256)S(1)} %reshape.169.slots_ref, f32[4,4,2,2,32,256]{5,4,3,2,1,0:T(8,128)S(1)} %copy-done, f32[4,4,2,2,32,256]{5,4,3,2,1,0:T(8,128)} %collective-permute-done.1.refs_1_, f32[8,128,1]{2,1,0:T(8,128)S(1)} %copy-done.10, ...), custom_call_target="tpu_custom_call", output_to_operand_aliasing={{}: (4, {})} | custom-call | flops 9663676416 | bytes 8388608 | tf_op jit(solution)/shard_map/pallas_call | solution.py:224
  241.8 5.9 %collective-permute-done.11.refs_1_ = f32[4,4,2,2,32,256]{5,4,3,2,1,0:T(8,128)} collective-permute-done((f32[4,4,2,2,32,256]{5,4,3,2,1,0:T(8,128)}, f32[4,4,2,2,32,256]{5,4,3,2,1,0:T(8,128)}, u32[]{:S(2)}, u32[]{:S(2)}) %collective-permute-start.11) | collective-permute-done | bytes 2097184 | tf_op jit(solution)/shard_map/ppermute | solution.py:14
  247.8 3.7 collective-permute-start.12
  251.5 18.8 %collective-permute-done.8.refs_1_ = f32[4,4,2,2,32,256]{5,4,3,2,1,0:T(8,128)} collective-permute-done((f32[4,4,2,2,32,256]{5,4,3,2,1,0:T(8,128)}, f32[4,4,2,2,32,256]{5,4,3,2,1,0:T(8,128)}, u32[]{:S(2)}, u32[]{:S(2)}) %collective-permute-start.8) | collective-permute-done | bytes 2097184 | tf_op jit(solution)/shard_map/ppermute | solution.py:14
  270.2 3.7 collective-permute-start.9
  273.9 11.2 %shard_map.50.refs_3_ = f32[66,8,2,128,128]{4,3,2,1,0:T(8,128)} custom-call(s32[132]{0:T(256)S(1)} %reshape.169.slots_ref, f32[4,4,2,2,32,256]{5,4,3,2,1,0:T(8,128)S(1)} %copy-done.9, f32[4,4,2,2,32,256]{5,4,3,2,1,0:T(8,128)} %collective-permute-done.11.refs_1_, f32[8,128,1]{2,1,0:T(8,128)S(1)} %copy.73.refs_2_, ...), custom_call_target="tpu_custom_call", output_to_operand_aliasing={{}: (4, {})} | custom-call | flops 9663676416 | bytes 8388608 | tf_op jit(solution)/shard_map/pallas_call | solution.py:224
  285.1 11.2 %shard_map.51.refs_3_ = f32[66,8,2,128,128]{4,3,2,1,0:T(8,128)} custom-call(s32[132]{0:T(256)S(1)} %reshape.169.slots_ref, f32[4,4,2,2,32,256]{5,4,3,2,1,0:T(8,128)S(1)} %copy-done.6, f32[4,4,2,2,32,256]{5,4,3,2,1,0:T(8,128)} %collective-permute-done.8.refs_1_, f32[8,128,1]{2,1,0:T(8,128)S(1)} %copy.73.refs_2_, ...), custom_call_target="tpu_custom_call", output_to_operand_aliasing={{}: (4, {})} | custom-call | flops 9663676416 | bytes 8388608 | tf_op jit(solution)/shard_map/pallas_call | solution.py:224
  296.4 0.0 collective-permute-done.5.refs_1_
  296.4 0.1 collective-permute-start.6
  296.5 11.2 %shard_map.52.refs_3_ = f32[66,8,2,128,128]{4,3,2,1,0:T(8,128)} custom-call(s32[132]{0:T(256)S(1)} %reshape.169.slots_ref, f32[4,4,2,2,32,256]{5,4,3,2,1,0:T(8,128)S(1)} %copy-done.3, f32[4,4,2,2,32,256]{5,4,3,2,1,0:T(8,128)} %collective-permute-done.5.refs_1_, f32[8,128,1]{2,1,0:T(8,128)S(1)} %copy.73.refs_2_, ...), custom_call_target="tpu_custom_call", output_to_operand_aliasing={{}: (4, {})} | custom-call | flops 9663676416 | bytes 8388608 | tf_op jit(solution)/shard_map/pallas_call | solution.py:224
  307.7 7.5 %collective-permute-done.2.refs_1_ = f32[4,4,2,2,32,256]{5,4,3,2,1,0:T(8,128)} collective-permute-done((f32[4,4,2,2,32,256]{5,4,3,2,1,0:T(8,128)}, f32[4,4,2,2,32,256]{5,4,3,2,1,0:T(8,128)}, u32[]{:S(2)}, u32[]{:S(2)}) %collective-permute-start.2) | collective-permute-done | bytes 2097184 | tf_op jit(solution)/shard_map/ppermute | solution.py:14
  315.2 3.7 collective-permute-start.3
  318.9 11.2 %shard_map.53.refs_3_ = f32[66,8,2,128,128]{4,3,2,1,0:T(8,128)} custom-call(s32[132]{0:T(256)S(1)} %reshape.169.slots_ref, f32[4,4,2,2,32,256]{5,4,3,2,1,0:T(8,128)S(1)} %copy-done, f32[4,4,2,2,32,256]{5,4,3,2,1,0:T(8,128)} %collective-permute-done.2.refs_1_, f32[8,128,1]{2,1,0:T(8,128)S(1)} %copy.73.refs_2_, ...), custom_call_target="tpu_custom_call", output_to_operand_aliasing={{}: (4, {})} | custom-call | flops 9663676416 | bytes 8388608 | tf_op jit(solution)/shard_map/pallas_call | solution.py:224
  330.1 7.5 %collective-permute-done.12.refs_1_ = f32[4,4,2,2,32,256]{5,4,3,2,1,0:T(8,128)} collective-permute-done((f32[4,4,2,2,32,256]{5,4,3,2,1,0:T(8,128)}, f32[4,4,2,2,32,256]{5,4,3,2,1,0:T(8,128)}, u32[]{:S(2)}, u32[]{:S(2)}) %collective-permute-start.12) | collective-permute-done | bytes 2097184 | tf_op jit(solution)/shard_map/ppermute | solution.py:14
  337.6 7.8 %shard_map.54.refs_3_ = f32[66,8,2,128,128]{4,3,2,1,0:T(8,128)} custom-call(s32[132]{0:T(256)S(1)} %reshape.169.slots_ref, f32[4,4,2,2,32,256]{5,4,3,2,1,0:T(8,128)S(1)} %copy-done.9, f32[4,4,2,2,32,256]{5,4,3,2,1,0:T(8,128)} %collective-permute-done.12.refs_1_, f32[8,128,1]{2,1,0:T(8,128)S(1)} %copy.77.refs_2_, ...), custom_call_target="tpu_custom_call", output_to_operand_aliasing={{}: (4, {})} | custom-call | flops 4831838208 | bytes 6291456 | tf_op jit(solution)/shard_map/pallas_call | solution.py:224
  345.5 14.6 %collective-permute-done.9.refs_1_ = f32[4,4,2,2,32,256]{5,4,3,2,1,0:T(8,128)} collective-permute-done((f32[4,4,2,2,32,256]{5,4,3,2,1,0:T(8,128)}, f32[4,4,2,2,32,256]{5,4,3,2,1,0:T(8,128)}, u32[]{:S(2)}, u32[]{:S(2)}) %collective-permute-start.9) | collective-permute-done | bytes 2097184 | tf_op jit(solution)/shard_map/ppermute | solution.py:14
  360.1 7.8 %shard_map.55.refs_3_ = f32[66,8,2,128,128]{4,3,2,1,0:T(8,128)} custom-call(s32[132]{0:T(256)S(1)} %reshape.169.slots_ref, f32[4,4,2,2,32,256]{5,4,3,2,1,0:T(8,128)S(1)} %copy-done.6, f32[4,4,2,2,32,256]{5,4,3,2,1,0:T(8,128)} %collective-permute-done.9.refs_1_, f32[8,128,1]{2,1,0:T(8,128)S(1)} %copy.77.refs_2_, ...), custom_call_target="tpu_custom_call", output_to_operand_aliasing={{}: (4, {})} | custom-call | flops 4831838208 | bytes 6291456 | tf_op jit(solution)/shard_map/pallas_call | solution.py:224
  367.9 14.6 %collective-permute-done.6.refs_1_ = f32[4,4,2,2,32,256]{5,4,3,2,1,0:T(8,128)} collective-permute-done((f32[4,4,2,2,32,256]{5,4,3,2,1,0:T(8,128)}, f32[4,4,2,2,32,256]{5,4,3,2,1,0:T(8,128)}, u32[]{:S(2)}, u32[]{:S(2)}) %collective-permute-start.6) | collective-permute-done | bytes 2097184 | tf_op jit(solution)/shard_map/ppermute | solution.py:14
  382.6 7.8 %shard_map.56.refs_3_ = f32[66,8,2,128,128]{4,3,2,1,0:T(8,128)} custom-call(s32[132]{0:T(256)S(1)} %reshape.169.slots_ref, f32[4,4,2,2,32,256]{5,4,3,2,1,0:T(8,128)S(1)} %copy-done.3, f32[4,4,2,2,32,256]{5,4,3,2,1,0:T(8,128)} %collective-permute-done.6.refs_1_, f32[8,128,1]{2,1,0:T(8,128)S(1)} %copy.77.refs_2_, ...), custom_call_target="tpu_custom_call", output_to_operand_aliasing={{}: (4, {})} | custom-call | flops 4831838208 | bytes 6291456 | tf_op jit(solution)/shard_map/pallas_call | solution.py:224
  390.4 14.6 %collective-permute-done.3.refs_1_ = f32[4,4,2,2,32,256]{5,4,3,2,1,0:T(8,128)} collective-permute-done((f32[4,4,2,2,32,256]{5,4,3,2,1,0:T(8,128)}, f32[4,4,2,2,32,256]{5,4,3,2,1,0:T(8,128)}, u32[]{:S(2)}, u32[]{:S(2)}) %collective-permute-start.3) | collective-permute-done | bytes 2097184 | tf_op jit(solution)/shard_map/ppermute | solution.py:14
  405.0 7.8 %shard_map.57 = f32[66,8,2,128,128]{4,3,2,1,0:T(8,128)} custom-call(s32[132]{0:T(256)S(1)} %reshape.169.slots_ref, f32[4,4,2,2,32,256]{5,4,3,2,1,0:T(8,128)S(1)} %copy-done, f32[4,4,2,2,32,256]{5,4,3,2,1,0:T(8,128)} %collective-permute-done.3.refs_1_, f32[8,128,1]{2,1,0:T(8,128)S(1)} %copy.77.refs_2_, ...), custom_call_target="tpu_custom_call", output_to_operand_aliasing={{}: (4, {})} | custom-call | flops 4831838208 | bytes 6291456 | tf_op jit(solution)/shard_map/pallas_call | solution.py:224
  (39 shorter events, 0.1 us)
Async XLA Ops:
  0.0 111.8 %copy-start.18 = (s32[64]{0:T(128)S(1)}, s32[64]{0:T(128)}, u32[]{:S(2)}) copy-start(s32[64]{0:T(128)} %param.5) | copy-start | bytes 772
  0.0 112.2 %copy-start.17 = (s32[66,2]{0,1:T(2,128)S(1)}, s32[66,2]{0,1:T(2,128)}, u32[]{:S(2)}) copy-start(s32[66,2]{0,1:T(2,128)} %param.4) | copy-start | bytes 1588
  107.8 72.4 %collective-permute-start = (f32[4,4,2,2,32,256]{5,4,3,2,1,0:T(8,128)}, f32[4,4,2,2,32,256]{5,4,3,2,1,0:T(8,128)}, u32[]{:S(2)}, u32[]{:S(2)}) collective-permute-start(f32[4,4,2,2,32,256]{5,4,3,2,1,0:T(8,128)} %get-tuple-element.12.refs_0_), channel_id=1, source_target_pairs={{0,7},{1,0},{2,1},{3,2},{4,3},{5,4},{6,5},{7,6},{8,15},{9,8},{10,9... | collective-permute-start | bytes 6291464 | tf_op jit(solution)/shard_map/ppermute | solution.py:14
  111.5 80.1 %collective-permute-start.10 = (f32[4,4,2,2,32,256]{5,4,3,2,1,0:T(8,128)}, f32[4,4,2,2,32,256]{5,4,3,2,1,0:T(8,128)}, u32[]{:S(2)}, u32[]{:S(2)}) collective-permute-start(f32[4,4,2,2,32,256]{5,4,3,2,1,0:T(8,128)} %get-tuple-element.18.refs_1_), channel_id=1, source_target_pairs={{0,7},{1,0},{2,1},{3,2},{4,3},{5,4},{6,5},{7,6},{8,15},{9,8},{10,9... | collective-permute-start | bytes 6291464 | tf_op jit(solution)/shard_map/ppermute | solution.py:14
  111.6 80.1 %collective-permute-start.7 = (f32[4,4,2,2,32,256]{5,4,3,2,1,0:T(8,128)}, f32[4,4,2,2,32,256]{5,4,3,2,1,0:T(8,128)}, u32[]{:S(2)}, u32[]{:S(2)}) collective-permute-start(f32[4,4,2,2,32,256]{5,4,3,2,1,0:T(8,128)} %get-tuple-element.16.refs_1_), channel_id=1, source_target_pairs={{0,7},{1,0},{2,1},{3,2},{4,3},{5,4},{6,5},{7,6},{8,15},{9,8},{10,9... | collective-permute-start | bytes 6291464 | tf_op jit(solution)/shard_map/ppermute | solution.py:14
  111.7 102.8 %collective-permute-start.4 = (f32[4,4,2,2,32,256]{5,4,3,2,1,0:T(8,128)}, f32[4,4,2,2,32,256]{5,4,3,2,1,0:T(8,128)}, u32[]{:S(2)}, u32[]{:S(2)}) collective-permute-start(f32[4,4,2,2,32,256]{5,4,3,2,1,0:T(8,128)} %get-tuple-element.14.refs_1_), channel_id=1, source_target_pairs={{0,7},{1,0},{2,1},{3,2},{4,3},{5,4},{6,5},{7,6},{8,15},{9,8},{10,9... | collective-permute-start | bytes 6291464 | tf_op jit(solution)/shard_map/ppermute | solution.py:14
  112.5 1.6 copy-start.7
  114.1 6.6 %copy-start.4 = (f32[4,4,2,2,32,256]{5,4,3,2,1,0:T(8,128)S(1)}, f32[4,4,2,2,32,256]{5,4,3,2,1,0:T(8,128)}, u32[]{:S(2)}) copy-start(f32[4,4,2,2,32,256]{5,4,3,2,1,0:T(8,128)} %get-tuple-element.15.refs_0_) | copy-start | bytes 6291460
  120.7 6.6 %copy-start.1 = (f32[4,4,2,2,32,256]{5,4,3,2,1,0:T(8,128)S(1)}, f32[4,4,2,2,32,256]{5,4,3,2,1,0:T(8,128)}, u32[]{:S(2)}) copy-start(f32[4,4,2,2,32,256]{5,4,3,2,1,0:T(8,128)} %get-tuple-element.13.refs_0_) | copy-start | bytes 6291460
  127.3 6.6 %copy-start = (f32[4,4,2,2,32,256]{5,4,3,2,1,0:T(8,128)S(1)}, f32[4,4,2,2,32,256]{5,4,3,2,1,0:T(8,128)}, u32[]{:S(2)}) copy-start(f32[4,4,2,2,32,256]{5,4,3,2,1,0:T(8,128)} %get-tuple-element.12.refs_0_) | copy-start | bytes 6291460
  140.8 1.6 copy-start.8
  142.4 1.6 copy-start.16
  144.0 10.2 %copy-start.11 = (f32[8,128,1]{2,1,0:T(8,128)}, f32[8,128,1]{2,1,0:T(8,128)S(1)}, u32[]{:S(2)}) copy-start(f32[8,128,1]{2,1,0:T(8,128)S(1)} %copy.65.refs_2_) | copy-start | bytes 12292
  144.0 10.2 %copy-start.5 = (f32[4,4,2,2,32,256]{5,4,3,2,1,0:T(8,128)S(1)}, f32[4,4,2,2,32,256]{5,4,3,2,1,0:T(8,128)}, u32[]{:S(2)}) copy-start(f32[4,4,2,2,32,256]{5,4,3,2,1,0:T(8,128)} %get-tuple-element.15.refs_0_) | copy-start | bytes 6291460
  144.0 10.2 %copy-start.15 = (f32[4,4,2,2,32,256]{5,4,3,2,1,0:T(8,128)S(1)}, f32[4,4,2,2,32,256]{5,4,3,2,1,0:T(8,128)}, u32[]{:S(2)}) copy-start(f32[4,4,2,2,32,256]{5,4,3,2,1,0:T(8,128)} %get-tuple-element.16.refs_1_) | copy-start | bytes 6291460
  165.8 1.6 copy-start.2
  167.4 1.0 copy-start.12
  168.5 1.6 copy-start.14
  170.1 10.3 %copy-start.13 = (f32[8,128,1]{2,1,0:T(8,128)S(1)}, f32[8,128,1]{2,1,0:T(8,128)}, u32[]{:S(2)}) copy-start(f32[8,128,1]{2,1,0:T(8,128)} %copy-done.11) | copy-start | bytes 12292
  180.2 11.8 %copy-start.9 = (f32[4,4,2,2,32,256]{5,4,3,2,1,0:T(8,128)S(1)}, f32[4,4,2,2,32,256]{5,4,3,2,1,0:T(8,128)}, u32[]{:S(2)}) copy-start(f32[4,4,2,2,32,256]{5,4,3,2,1,0:T(8,128)} %get-tuple-element.17.refs_0_) | copy-start | bytes 6291460
  180.2 11.8 %copy-start.10 = (f32[8,128,1]{2,1,0:T(8,128)S(1)}, f32[8,128,1]{2,1,0:T(8,128)}, u32[]{:S(2)}) copy-start(f32[8,128,1]{2,1,0:T(8,128)} %copy.69.refs_2_) | copy-start | bytes 12292
  180.2 46.6 %collective-permute-start.1 = (f32[4,4,2,2,32,256]{5,4,3,2,1,0:T(8,128)}, f32[4,4,2,2,32,256]{5,4,3,2,1,0:T(8,128)}, u32[]{:S(2)}, u32[]{:S(2)}) collective-permute-start(f32[4,4,2,2,32,256]{5,4,3,2,1,0:T(8,128)} %collective-permute-done.refs_1_), channel_id=1, source_target_pairs={{0,7},{1,0},{2,1},{3,2},{4,3},{5,4},{6,5},{7,6},{8,15},{9,8},{10,9... | collective-permute-start | bytes 6291464 | tf_op jit(solution)/shard_map/ppermute | solution.py:14
  191.6 11.6 %copy-start.6 = (f32[4,4,2,2,32,256]{5,4,3,2,1,0:T(8,128)S(1)}, f32[4,4,2,2,32,256]{5,4,3,2,1,0:T(8,128)}, u32[]{:S(2)}) copy-start(f32[4,4,2,2,32,256]{5,4,3,2,1,0:T(8,128)} %get-tuple-element.15.refs_0_) | copy-start | bytes 6291460
  191.6 56.1 %collective-permute-start.11 = (f32[4,4,2,2,32,256]{5,4,3,2,1,0:T(8,128)}, f32[4,4,2,2,32,256]{5,4,3,2,1,0:T(8,128)}, u32[]{:S(2)}, u32[]{:S(2)}) collective-permute-start(f32[4,4,2,2,32,256]{5,4,3,2,1,0:T(8,128)} %collective-permute-done.10.refs_1_), channel_id=1, source_target_pairs={{0,7},{1,0},{2,1},{3,2},{4,3},{5,4},{6,5},{7,6},{8,15},{9,8},{10,9... | collective-permute-start | bytes 6291464 | tf_op jit(solution)/shard_map/ppermute | solution.py:14
  191.7 78.5 %collective-permute-start.8 = (f32[4,4,2,2,32,256]{5,4,3,2,1,0:T(8,128)}, f32[4,4,2,2,32,256]{5,4,3,2,1,0:T(8,128)}, u32[]{:S(2)}, u32[]{:S(2)}) collective-permute-start(f32[4,4,2,2,32,256]{5,4,3,2,1,0:T(8,128)} %collective-permute-done.7.refs_1_), channel_id=1, source_target_pairs={{0,7},{1,0},{2,1},{3,2},{4,3},{5,4},{6,5},{7,6},{8,15},{9,8},{10,9... | collective-permute-start | bytes 6291464 | tf_op jit(solution)/shard_map/ppermute | solution.py:14
  203.2 12.5 %copy-start.3 = (f32[4,4,2,2,32,256]{5,4,3,2,1,0:T(8,128)S(1)}, f32[4,4,2,2,32,256]{5,4,3,2,1,0:T(8,128)}, u32[]{:S(2)}) copy-start(f32[4,4,2,2,32,256]{5,4,3,2,1,0:T(8,128)} %get-tuple-element.13.refs_0_) | copy-start | bytes 6291460
  214.4 82.0 %collective-permute-start.5 = (f32[4,4,2,2,32,256]{5,4,3,2,1,0:T(8,128)}, f32[4,4,2,2,32,256]{5,4,3,2,1,0:T(8,128)}, u32[]{:S(2)}, u32[]{:S(2)}) collective-permute-start(f32[4,4,2,2,32,256]{5,4,3,2,1,0:T(8,128)} %collective-permute-done.4.refs_1_), channel_id=1, source_target_pairs={{0,7},{1,0},{2,1},{3,2},{4,3},{5,4},{6,5},{7,6},{8,15},{9,8},{10,9... | collective-permute-start | bytes 6291464 | tf_op jit(solution)/shard_map/ppermute | solution.py:14
  226.9 88.3 %collective-permute-start.2 = (f32[4,4,2,2,32,256]{5,4,3,2,1,0:T(8,128)}, f32[4,4,2,2,32,256]{5,4,3,2,1,0:T(8,128)}, u32[]{:S(2)}, u32[]{:S(2)}) collective-permute-start(f32[4,4,2,2,32,256]{5,4,3,2,1,0:T(8,128)} %collective-permute-done.1.refs_1_), channel_id=1, source_target_pairs={{0,7},{1,0},{2,1},{3,2},{4,3},{5,4},{6,5},{7,6},{8,15},{9,8},{10,9... | collective-permute-start | bytes 6291464 | tf_op jit(solution)/shard_map/ppermute | solution.py:14
  247.8 89.9 %collective-permute-start.12 = (f32[4,4,2,2,32,256]{5,4,3,2,1,0:T(8,128)}, f32[4,4,2,2,32,256]{5,4,3,2,1,0:T(8,128)}, u32[]{:S(2)}, u32[]{:S(2)}) collective-permute-start(f32[4,4,2,2,32,256]{5,4,3,2,1,0:T(8,128)} %collective-permute-done.11.refs_1_), channel_id=1, source_target_pairs={{0,7},{1,0},{2,1},{3,2},{4,3},{5,4},{6,5},{7,6},{8,15},{9,8},{10,9... | collective-permute-start | bytes 6291464 | tf_op jit(solution)/shard_map/ppermute | solution.py:14
  270.2 89.9 %collective-permute-start.9 = (f32[4,4,2,2,32,256]{5,4,3,2,1,0:T(8,128)}, f32[4,4,2,2,32,256]{5,4,3,2,1,0:T(8,128)}, u32[]{:S(2)}, u32[]{:S(2)}) collective-permute-start(f32[4,4,2,2,32,256]{5,4,3,2,1,0:T(8,128)} %collective-permute-done.8.refs_1_), channel_id=1, source_target_pairs={{0,7},{1,0},{2,1},{3,2},{4,3},{5,4},{6,5},{7,6},{8,15},{9,8},{10,9... | collective-permute-start | bytes 6291464 | tf_op jit(solution)/shard_map/ppermute | solution.py:14
  296.4 86.2 %collective-permute-start.6 = (f32[4,4,2,2,32,256]{5,4,3,2,1,0:T(8,128)}, f32[4,4,2,2,32,256]{5,4,3,2,1,0:T(8,128)}, u32[]{:S(2)}, u32[]{:S(2)}) collective-permute-start(f32[4,4,2,2,32,256]{5,4,3,2,1,0:T(8,128)} %collective-permute-done.5.refs_1_), channel_id=1, source_target_pairs={{0,7},{1,0},{2,1},{3,2},{4,3},{5,4},{6,5},{7,6},{8,15},{9,8},{10,9... | collective-permute-start | bytes 6291464 | tf_op jit(solution)/shard_map/ppermute | solution.py:14
  315.2 89.9 %collective-permute-start.3 = (f32[4,4,2,2,32,256]{5,4,3,2,1,0:T(8,128)}, f32[4,4,2,2,32,256]{5,4,3,2,1,0:T(8,128)}, u32[]{:S(2)}, u32[]{:S(2)}) collective-permute-start(f32[4,4,2,2,32,256]{5,4,3,2,1,0:T(8,128)} %collective-permute-done.2.refs_1_), channel_id=1, source_target_pairs={{0,7},{1,0},{2,1},{3,2},{4,3},{5,4},{6,5},{7,6},{8,15},{9,8},{10,9... | collective-permute-start | bytes 6291464 | tf_op jit(solution)/shard_map/ppermute | solution.py:14

commit v3 on v2

--- a/solution.py
+++ b/solution.py
@@ -16,8 +16,8 @@
 
 def turn_kernel(chunks, volts, *refs):
     own = refs[:chunks]
-    far = refs[chunks : 2 * chunks - 1]
-    local_sem, send_sem, recv_sem, pass_send, pass_recv = refs[2 * chunks - 1 :]
+    far = refs[chunks : 2 * chunks]
+    local_sem, send_sem, recv_sem, pass_send, pass_recv = refs[2 * chunks :]
     count = lax.axis_size("freq")
     me = lax.axis_index("freq")
     blk_count = lax.axis_size("blk")
@@ -41,44 +41,48 @@
         )
     pl.semaphore_wait(barrier, count + 1)
 
-    def part(device, g):
-        return volts.at[:, pl.ds(device * chan_dev + g * per_chunk, per_chunk)]
-
-    kept, sent, passed = [], [], []
-    for g in range(chunks):
-        kept.append(pltpu.make_async_copy(part(me, g), own[g].at[me], local_sem.at[g]))
-        kept[g].start()
-        sent.append([])
+    def begin(unit):
+        held = own[unit // per_chunk].at[me, :, unit % per_chunk]
+        kept = pltpu.make_async_copy(
+            volts.at[:, me * chan_dev + unit], held, local_sem.at[unit]
+        )
+        sent = []
         for shift in range(1, count):
             peer = lax.rem(me + shift, count)
             copy = pltpu.make_async_remote_copy(
-                src_ref=part(peer, g),
-                dst_ref=own[g].at[me],
-                send_sem=send_sem.at[g, shift - 1],
-                recv_sem=recv_sem.at[g, shift - 1],
+                src_ref=volts.at[:, peer * chan_dev + unit],
+                dst_ref=held,
+                send_sem=send_sem.at[unit, shift - 1],
+                recv_sem=recv_sem.at[unit, shift - 1],
                 device_id=(peer, here),
                 device_id_type=pl.DeviceIdType.MESH,
             )
             copy.start()
-            sent[g].append(copy)
-    for g in range(chunks):
-        kept[g].wait()
-        for copy in sent[g]:
+            sent.append(copy)
+        kept.start()
+        return kept, sent
+
+    passed = []
+    kept, sent = begin(0)
+    for unit in range(chan_dev):
+        for copy in sent:
+            copy.wait_send()
+        now_kept, now_sent = kept, sent
+        if unit + 1 < chan_dev:
+            kept, sent = begin(unit + 1)
+        now_kept.wait()
+        for copy in now_sent:
             copy.wait_recv()
-        if g < chunks - 1:
-            copy = pltpu.make_async_remote_copy(
-                src_ref=own[g],
-                dst_ref=far[g],
-                send_sem=pass_send.at[g],
-                recv_sem=pass_recv.at[g],
-                device_id=(me, before),
-                device_id_type=pl.DeviceIdType.MESH,
-            )
-            copy.start()
-            passed.append(copy)
-    for g in range(chunks):
-        for copy in sent[g]:
-            copy.wait_send()
+        copy = pltpu.make_async_remote_copy(
+            src_ref=own[unit // per_chunk].at[:, :, unit % per_chunk],
+            dst_ref=far[unit // per_chunk].at[:, :, unit % per_chunk],
+            send_sem=pass_send.at[unit],
+            recv_sem=pass_recv.at[unit],
+            device_id=(me, before),
+            device_id_type=pl.DeviceIdType.MESH,
+        )
+        copy.start()
+        passed.append(copy)
     for copy in passed:
         copy.wait()
 
@@ -86,23 +90,24 @@
 def turned(voltages, chunks):
     count = lax.axis_size("freq")
     per_dev, chans, _, rows, samples = voltages.shape
-    per_chunk = chans // count // chunks
+    chan_dev = chans // count
+    per_chunk = chan_dev // chunks
     piece = jax.ShapeDtypeStruct(
         (count, per_dev, per_chunk, 2, rows, samples), voltages.dtype
     )
     any_spec = pl.BlockSpec(memory_space=pl.ANY)
-    made = 2 * chunks - 1
+    made = 2 * chunks
     outs = pl.pallas_call(
         functools.partial(turn_kernel, chunks),
         out_shape=[piece] * made,
         in_specs=[any_spec],
         out_specs=[any_spec] * made,
         scratch_shapes=[
-            pltpu.SemaphoreType.DMA((chunks,)),
-            pltpu.SemaphoreType.DMA((chunks, count - 1)),
-            pltpu.SemaphoreType.DMA((chunks, count - 1)),
-            pltpu.SemaphoreType.DMA((chunks,)),
-            pltpu.SemaphoreType.DMA((chunks,)),
+            pltpu.SemaphoreType.DMA((chan_dev,)),
+            pltpu.SemaphoreType.DMA((chan_dev, count - 1)),
+            pltpu.SemaphoreType.DMA((chan_dev, count - 1)),
+            pltpu.SemaphoreType.DMA((chan_dev,)),
+            pltpu.SemaphoreType.DMA((chan_dev,)),
         ],
         compiler_params=pltpu.CompilerParams(collective_id=0, has_side_effects=True),
         cost_estimate=pl.CostEstimate(
@@ -259,12 +264,8 @@
         visibility = place_group(
             visibility, out_type, slots, 0, own_count, g * per_chunk, [own[g]], own_keep
         )
-    far = own
     for step in range(1, half + 1):
-        far = [
-            first_hop[g] if step == 1 and g < chunks - 1 else passed_along(far[g], "blk")
-            for g in range(chunks)
-        ]
+        far = first_hop if step == 1 else [passed_along(piece, "blk") for piece in far]
         both_keep = jnp.concatenate([own_keep, kept(step)], axis=0)
         for g in range(chunks):
             visibility = place_group(

time: 414 us -> 399 us (0.964)
  waiting for transfers between devices: 83.6 us -> 70 us
  Pallas kernels: 297 us -> 304 us
  local copies, waits for them, and re-layouts: 11.1 us -> 6.53 us
    ppermute x13 -> x12, waiting for transfers between devices: 83.6 us -> 70 us  [passed_along(): return lax.ppermute(value, axis, pairs)]
    pallas_call x1, Pallas kernels: 108 us -> 116 us  [turned(): pl.pallas_call(functools.partial(turn_kernel, chunks), out_shape=[piece]...]
    unnamed x38 -> x36, local copies, waits for them, and re-layouts: 9.04 us -> 4.45 us
    ppermute x13 -> x12, starting transfers between devices: 20.5 us -> 16.6 us  [passed_along(): return lax.ppermute(value, axis, pairs)]
  transfers between devices with their start and end apart: 13 -> 12, of which waited for: 7 -> 6; matrix products, arithmetic and copies ran while one was open for 1% -> 1% of each run, Pallas kernels for 44% -> 45%
where the time goes in v3:
time: 399 us; the launch traced here: 398 us
  Pallas kernels  304 us (76%)
  waiting for transfers between devices  70 us (18%)
  starting transfers between devices  16.6 us (4%)
  local copies, waits for them, and re-layouts  6.53 us (2%)
    pallas_call x20, Pallas kernels, place_group(): return call(slots, *sets, keep, *([prev] if has_prev else []))  188 us
    pallas_call x1, Pallas kernels, turned(): pl.pallas_call(functools.partial(turn_kernel, chunks), out_shape=[piece]...  116 us
    ppermute x12, waiting for transfers between devices, passed_along(): return lax.ppermute(value, axis, pairs)  70 us
    ppermute x12, starting transfers between devices, passed_along(): return lax.ppermute(value, axis, pairs)  16.6 us
  transfers between devices with their start and end apart: 12, of which 6 were waited for; matrix products, arithmetic and copies ran while one was open for 1% of the time, Pallas kernels for 45%

profile of v3, /device:TPU:0, one launch (start us, length us, event | category | flops | bytes accessed | tf_op | source)
XLA Modules:
  0.0 398.4 jit_solution(18324391441422526092)
XLA Ops:
  0.0 115.6 %shard_map.37 = (f32[4,4,2,2,32,256]{5,4,3,2,1,0:T(8,128)}, f32[4,4,2,2,32,256]{5,4,3,2,1,0:T(8,128)}, f32[4,4,2,2,32,256]{5,4,3,2,1,0:T(8,128)}, f32[4,4,2,2,32...) custom-call(f32[4,32,2,32,256]{4,3,2,1,0:T(8,128)} %volts.1), custom_call_target="tpu_custom_call" | custom-call | bytes 16777216 | tf_op jit(solution)/shard_map/pallas_call | solution.py:100
  115.6 3.8 collective-permute-start.9
  119.4 0.1 collective-permute-start.6
  119.4 0.1 collective-permute-start.3
  119.5 0.1 collective-permute-start
  119.7 0.2 compare_reduce_fusion
  119.9 0.1 copy.61.refs_1_
  120.0 0.0 copy-done.16
  120.0 0.1 copy.57
  120.2 0.1 reshape.169.slots_ref
  120.3 0.6 pad_maximum_fusion
  120.9 0.2 copy.65.refs_2_
  121.2 1.6 copy-done.5
  122.8 6.6 %shard_map.38.refs_2_ = f32[66,8,2,128,128]{4,3,2,1,0:T(8,128)} custom-call(s32[132]{0:T(256)S(1)} %reshape.169.slots_ref, f32[4,4,2,2,32,256]{5,4,3,2,1,0:T(8,128)S(1)} %copy-done.5, f32[4,128,1]{2,1,0:T(8,128)S(1)} %copy.61.refs_1_), custom_call_target="tpu_custom_call" | custom-call | flops 6039797760 | bytes 4718592 | tf_op jit(solution)/shard_map/pallas_call | solution.py:229
  129.4 0.0 copy-done.3
  129.4 0.0 copy-start.1
  129.4 6.6 %shard_map.39.refs_2_ = f32[66,8,2,128,128]{4,3,2,1,0:T(8,128)} custom-call(s32[132]{0:T(256)S(1)} %reshape.169.slots_ref, f32[4,4,2,2,32,256]{5,4,3,2,1,0:T(8,128)S(1)} %copy-done.3, f32[4,128,1]{2,1,0:T(8,128)S(1)} %copy.61.refs_1_, f32[66,8,2,128,128]{4,3,2,1,0:T(8,128)} %shard_map.38.refs_2_), custom_call_target="tpu_custom_call", output_to_operand_aliasing={{}: (3, {})} | custom-call | flops 6039797760 | bytes 4718592 | tf_op jit(solution)/shard_map/pallas_call | solution.py:229
  136.0 6.6 %shard_map.40.refs_2_ = f32[66,8,2,128,128]{4,3,2,1,0:T(8,128)} custom-call(s32[132]{0:T(256)S(1)} %reshape.169.slots_ref, f32[4,4,2,2,32,256]{5,4,3,2,1,0:T(8,128)S(1)} %copy-done.1, f32[4,128,1]{2,1,0:T(8,128)S(1)} %copy.61.refs_1_, f32[66,8,2,128,128]{4,3,2,1,0:T(8,128)} %shard_map.39.refs_2_), custom_call_target="tpu_custom_call", output_to_operand_aliasing={{}: (3, {})} | custom-call | flops 6039797760 | bytes 4718592 | tf_op jit(solution)/shard_map/pallas_call | solution.py:229
  142.6 0.0 copy-done
  142.6 0.0 copy-start.12
  142.7 6.6 %shard_map.41.refs_3_ = f32[66,8,2,128,128]{4,3,2,1,0:T(8,128)} custom-call(s32[132]{0:T(256)S(1)} %reshape.169.slots_ref, f32[4,4,2,2,32,256]{5,4,3,2,1,0:T(8,128)S(1)} %copy-done, f32[4,128,1]{2,1,0:T(8,128)S(1)} %copy.61.refs_1_, f32[66,8,2,128,128]{4,3,2,1,0:T(8,128)} %shard_map.40.refs_2_), custom_call_target="tpu_custom_call", output_to_operand_aliasing={{}: (3, {})} | custom-call | flops 6039797760 | bytes 4718592 | tf_op jit(solution)/shard_map/pallas_call | solution.py:229
  149.3 10.1 %shard_map.42.refs_3_ = f32[66,8,2,128,128]{4,3,2,1,0:T(8,128)} custom-call(s32[132]{0:T(256)S(1)} %reshape.169.slots_ref, f32[4,4,2,2,32,256]{5,4,3,2,1,0:T(8,128)S(1)} %copy-done.5, f32[4,4,2,2,32,256]{5,4,3,2,1,0:T(8,128)S(1)} %copy-done.12, f32[8,128,1]{2,1,0:T(8,128)S(1)} %copy.65.refs_2_, ...), custom_call_target="tpu_custom_call", output_to_operand_aliasing={{}: (4, {})} | custom-call | flops 9663676416 | bytes 8388608 | tf_op jit(solution)/shard_map/pallas_call | solution.py:229
  159.5 10.1 %shard_map.43.refs_3_ = f32[66,8,2,128,128]{4,3,2,1,0:T(8,128)} custom-call(s32[132]{0:T(256)S(1)} %reshape.169.slots_ref, f32[4,4,2,2,32,256]{5,4,3,2,1,0:T(8,128)S(1)} %copy-done.3, f32[4,4,2,2,32,256]{5,4,3,2,1,0:T(8,128)S(1)} %copy-done.11, f32[8,128,1]{2,1,0:T(8,128)S(1)} %copy.65.refs_2_, ...), custom_call_target="tpu_custom_call", output_to_operand_aliasing={{}: (4, {})} | custom-call | flops 9663676416 | bytes 8388608 | tf_op jit(solution)/shard_map/pallas_call | solution.py:229
  169.6 0.0 copy-done.10
  169.6 0.0 copy-start.9
  169.6 10.1 %shard_map.44.refs_3_ = f32[66,8,2,128,128]{4,3,2,1,0:T(8,128)} custom-call(s32[132]{0:T(256)S(1)} %reshape.169.slots_ref, f32[4,4,2,2,32,256]{5,4,3,2,1,0:T(8,128)S(1)} %copy-done.1, f32[4,4,2,2,32,256]{5,4,3,2,1,0:T(8,128)S(1)} %copy-done.10, f32[8,128,1]{2,1,0:T(8,128)S(1)} %copy.65.refs_2_, ...), custom_call_target="tpu_custom_call", output_to_operand_aliasing={{}: (4, {})} | custom-call | flops 9663676416 | bytes 8388608 | tf_op jit(solution)/shard_map/pallas_call | solution.py:229
  179.8 10.2 %shard_map.45.refs_3_ = f32[66,8,2,128,128]{4,3,2,1,0:T(8,128)} custom-call(s32[132]{0:T(256)S(1)} %reshape.169.slots_ref, f32[4,4,2,2,32,256]{5,4,3,2,1,0:T(8,128)S(1)} %copy-done, f32[4,4,2,2,32,256]{5,4,3,2,1,0:T(8,128)S(1)} %copy-done.9, f32[8,128,1]{2,1,0:T(8,128)S(1)} %copy.65.refs_2_, ...), custom_call_target="tpu_custom_call", output_to_operand_aliasing={{}: (4, {})} | custom-call | flops 9663676416 | bytes 8388608 | tf_op jit(solution)/shard_map/pallas_call | solution.py:229
  190.0 1.0 copy.69.refs_2_
  191.0 0.2 copy.73.refs_2_
  191.2 0.2 copy.77.refs_2_
  191.5 0.0 collective-permute-done.9.refs_1_
  191.5 0.1 collective-permute-start.10
  191.6 0.0 collective-permute-done.6.refs_1_
  191.6 0.2 collective-permute-start.7
  191.8 1.8 copy-done.6
  193.6 1.0 copy-done.7
  194.6 11.2 %shard_map.46.refs_3_ = f32[66,8,2,128,128]{4,3,2,1,0:T(8,128)} custom-call(s32[132]{0:T(256)S(1)} %reshape.169.slots_ref, f32[4,4,2,2,32,256]{5,4,3,2,1,0:T(8,128)S(1)} %copy-done.6, f32[4,4,2,2,32,256]{5,4,3,2,1,0:T(8,128)} %collective-permute-done.9.refs_1_, f32[8,128,1]{2,1,0:T(8,128)S(1)} %copy-done.7, ...), custom_call_target="tpu_custom_call", output_to_operand_aliasing={{}: (4, {})} | custom-call | flops 9663676416 | bytes 8388608 | tf_op jit(solution)/shard_map/pallas_call | solution.py:229
  205.9 11.2 %shard_map.47.refs_3_ = f32[66,8,2,128,128]{4,3,2,1,0:T(8,128)} custom-call(s32[132]{0:T(256)S(1)} %reshape.169.slots_ref, f32[4,4,2,2,32,256]{5,4,3,2,1,0:T(8,128)S(1)} %copy-done.4, f32[4,4,2,2,32,256]{5,4,3,2,1,0:T(8,128)} %collective-permute-done.6.refs_1_, f32[8,128,1]{2,1,0:T(8,128)S(1)} %copy-done.8, ...), custom_call_target="tpu_custom_call", output_to_operand_aliasing={{}: (4, {})} | custom-call | flops 9663676416 | bytes 8388608 | tf_op jit(solution)/shard_map/pallas_call | solution.py:229
  217.1 0.0 collective-permute-done.3.refs_1_
  217.1 0.1 collective-permute-start.4
  217.2 0.0 collective-permute-done.refs_1_
  217.2 1.0 collective-permute-start.1
  218.3 11.2 %shard_map.48.refs_3_ = f32[66,8,2,128,128]{4,3,2,1,0:T(8,128)} custom-call(s32[132]{0:T(256)S(1)} %reshape.169.slots_ref, f32[4,4,2,2,32,256]{5,4,3,2,1,0:T(8,128)S(1)} %copy-done.2, f32[4,4,2,2,32,256]{5,4,3,2,1,0:T(8,128)} %collective-permute-done.3.refs_1_, f32[8,128,1]{2,1,0:T(8,128)S(1)} %copy-done.8, ...), custom_call_target="tpu_custom_call", output_to_operand_aliasing={{}: (4, {})} | custom-call | flops 9663676416 | bytes 8388608 | tf_op jit(solution)/shard_map/pallas_call | solution.py:229
  229.5 11.2 %shard_map.49.refs_3_ = f32[66,8,2,128,128]{4,3,2,1,0:T(8,128)} custom-call(s32[132]{0:T(256)S(1)} %reshape.169.slots_ref, f32[4,4,2,2,32,256]{5,4,3,2,1,0:T(8,128)S(1)} %copy-done, f32[4,4,2,2,32,256]{5,4,3,2,1,0:T(8,128)} %collective-permute-done.refs_1_, f32[8,128,1]{2,1,0:T(8,128)S(1)} %copy-done.8, ...), custom_call_target="tpu_custom_call", output_to_operand_aliasing={{}: (4, {})} | custom-call | flops 9663676416 | bytes 8388608 | tf_op jit(solution)/shard_map/pallas_call | solution.py:229
  240.7 0.0 collective-permute-done.10.refs_1_
  240.7 3.8 collective-permute-start.11
  244.5 11.1 %collective-permute-done.7.refs_1_ = f32[4,4,2,2,32,256]{5,4,3,2,1,0:T(8,128)} collective-permute-done((f32[4,4,2,2,32,256]{5,4,3,2,1,0:T(8,128)}, f32[4,4,2,2,32,256]{5,4,3,2,1,0:T(8,128)}, u32[]{:S(2)}, u32[]{:S(2)}) %collective-permute-start.7) | collective-permute-done | bytes 2097184 | tf_op jit(solution)/shard_map/ppermute | solution.py:14
  255.6 3.7 collective-permute-start.8
  259.3 11.2 %shard_map.50.refs_3_ = f32[66,8,2,128,128]{4,3,2,1,0:T(8,128)} custom-call(s32[132]{0:T(256)S(1)} %reshape.169.slots_ref, f32[4,4,2,2,32,256]{5,4,3,2,1,0:T(8,128)S(1)} %copy-done.6, f32[4,4,2,2,32,256]{5,4,3,2,1,0:T(8,128)} %collective-permute-done.10.refs_1_, f32[8,128,1]{2,1,0:T(8,128)S(1)} %copy.73.refs_2_, ...), custom_call_target="tpu_custom_call", output_to_operand_aliasing={{}: (4, {})} | custom-call | flops 9663676416 | bytes 8388608 | tf_op jit(solution)/shard_map/pallas_call | solution.py:229
  270.5 11.2 %shard_map.51.refs_3_ = f32[66,8,2,128,128]{4,3,2,1,0:T(8,128)} custom-call(s32[132]{0:T(256)S(1)} %reshape.169.slots_ref, f32[4,4,2,2,32,256]{5,4,3,2,1,0:T(8,128)S(1)} %copy-done.4, f32[4,4,2,2,32,256]{5,4,3,2,1,0:T(8,128)} %collective-permute-done.7.refs_1_, f32[8,128,1]{2,1,0:T(8,128)S(1)} %copy.73.refs_2_, ...), custom_call_target="tpu_custom_call", output_to_operand_aliasing={{}: (4, {})} | custom-call | flops 9663676416 | bytes 8388608 | tf_op jit(solution)/shard_map/pallas_call | solution.py:229
  281.7 0.0 collective-permute-done.4.refs_1_
  281.7 0.1 collective-permute-start.5
  281.8 11.2 %shard_map.52.refs_3_ = f32[66,8,2,128,128]{4,3,2,1,0:T(8,128)} custom-call(s32[132]{0:T(256)S(1)} %reshape.169.slots_ref, f32[4,4,2,2,32,256]{5,4,3,2,1,0:T(8,128)S(1)} %copy-done.2, f32[4,4,2,2,32,256]{5,4,3,2,1,0:T(8,128)} %collective-permute-done.4.refs_1_, f32[8,128,1]{2,1,0:T(8,128)S(1)} %copy.73.refs_2_, ...), custom_call_target="tpu_custom_call", output_to_operand_aliasing={{}: (4, {})} | custom-call | flops 9663676416 | bytes 8388608 | tf_op jit(solution)/shard_map/pallas_call | solution.py:229
  293.0 7.5 %collective-permute-done.1.refs_1_ = f32[4,4,2,2,32,256]{5,4,3,2,1,0:T(8,128)} collective-permute-done((f32[4,4,2,2,32,256]{5,4,3,2,1,0:T(8,128)}, f32[4,4,2,2,32,256]{5,4,3,2,1,0:T(8,128)}, u32[]{:S(2)}, u32[]{:S(2)}) %collective-permute-start.1) | collective-permute-done | bytes 2097184 | tf_op jit(solution)/shard_map/ppermute | solution.py:14
  300.5 3.7 collective-permute-start.2
  304.2 11.2 %shard_map.53.refs_3_ = f32[66,8,2,128,128]{4,3,2,1,0:T(8,128)} custom-call(s32[132]{0:T(256)S(1)} %reshape.169.slots_ref, f32[4,4,2,2,32,256]{5,4,3,2,1,0:T(8,128)S(1)} %copy-done, f32[4,4,2,2,32,256]{5,4,3,2,1,0:T(8,128)} %collective-permute-done.1.refs_1_, f32[8,128,1]{2,1,0:T(8,128)S(1)} %copy.73.refs_2_, ...), custom_call_target="tpu_custom_call", output_to_operand_aliasing={{}: (4, {})} | custom-call | flops 9663676416 | bytes 8388608 | tf_op jit(solution)/shard_map/pallas_call | solution.py:229
  315.4 7.6 %collective-permute-done.11.refs_1_ = f32[4,4,2,2,32,256]{5,4,3,2,1,0:T(8,128)} collective-permute-done((f32[4,4,2,2,32,256]{5,4,3,2,1,0:T(8,128)}, f32[4,4,2,2,32,256]{5,4,3,2,1,0:T(8,128)}, u32[]{:S(2)}, u32[]{:S(2)}) %collective-permute-start.11) | collective-permute-done | bytes 2097184 | tf_op jit(solution)/shard_map/ppermute | solution.py:14
  323.0 7.8 %shard_map.54.refs_3_ = f32[66,8,2,128,128]{4,3,2,1,0:T(8,128)} custom-call(s32[132]{0:T(256)S(1)} %reshape.169.slots_ref, f32[4,4,2,2,32,256]{5,4,3,2,1,0:T(8,128)S(1)} %copy-done.6, f32[4,4,2,2,32,256]{5,4,3,2,1,0:T(8,128)} %collective-permute-done.11.refs_1_, f32[8,128,1]{2,1,0:T(8,128)S(1)} %copy.77.refs_2_, ...), custom_call_target="tpu_custom_call", output_to_operand_aliasing={{}: (4, {})} | custom-call | flops 4831838208 | bytes 6291456 | tf_op jit(solution)/shard_map/pallas_call | solution.py:229
  330.9 14.6 %collective-permute-done.8.refs_1_ = f32[4,4,2,2,32,256]{5,4,3,2,1,0:T(8,128)} collective-permute-done((f32[4,4,2,2,32,256]{5,4,3,2,1,0:T(8,128)}, f32[4,4,2,2,32,256]{5,4,3,2,1,0:T(8,128)}, u32[]{:S(2)}, u32[]{:S(2)}) %collective-permute-start.8) | collective-permute-done | bytes 2097184 | tf_op jit(solution)/shard_map/ppermute | solution.py:14
  345.5 7.9 %shard_map.55.refs_3_ = f32[66,8,2,128,128]{4,3,2,1,0:T(8,128)} custom-call(s32[132]{0:T(256)S(1)} %reshape.169.slots_ref, f32[4,4,2,2,32,256]{5,4,3,2,1,0:T(8,128)S(1)} %copy-done.4, f32[4,4,2,2,32,256]{5,4,3,2,1,0:T(8,128)} %collective-permute-done.8.refs_1_, f32[8,128,1]{2,1,0:T(8,128)S(1)} %copy.77.refs_2_, ...), custom_call_target="tpu_custom_call", output_to_operand_aliasing={{}: (4, {})} | custom-call | flops 4831838208 | bytes 6291456 | tf_op jit(solution)/shard_map/pallas_call | solution.py:229
  353.3 14.6 %collective-permute-done.5.refs_1_ = f32[4,4,2,2,32,256]{5,4,3,2,1,0:T(8,128)} collective-permute-done((f32[4,4,2,2,32,256]{5,4,3,2,1,0:T(8,128)}, f32[4,4,2,2,32,256]{5,4,3,2,1,0:T(8,128)}, u32[]{:S(2)}, u32[]{:S(2)}) %collective-permute-start.5) | collective-permute-done | bytes 2097184 | tf_op jit(solution)/shard_map/ppermute | solution.py:14
  367.9 7.8 %shard_map.56.refs_3_ = f32[66,8,2,128,128]{4,3,2,1,0:T(8,128)} custom-call(s32[132]{0:T(256)S(1)} %reshape.169.slots_ref, f32[4,4,2,2,32,256]{5,4,3,2,1,0:T(8,128)S(1)} %copy-done.2, f32[4,4,2,2,32,256]{5,4,3,2,1,0:T(8,128)} %collective-permute-done.5.refs_1_, f32[8,128,1]{2,1,0:T(8,128)S(1)} %copy.77.refs_2_, ...), custom_call_target="tpu_custom_call", output_to_operand_aliasing={{}: (4, {})} | custom-call | flops 4831838208 | bytes 6291456 | tf_op jit(solution)/shard_map/pallas_call | solution.py:229
  375.8 14.6 %collective-permute-done.2.refs_1_ = f32[4,4,2,2,32,256]{5,4,3,2,1,0:T(8,128)} collective-permute-done((f32[4,4,2,2,32,256]{5,4,3,2,1,0:T(8,128)}, f32[4,4,2,2,32,256]{5,4,3,2,1,0:T(8,128)}, u32[]{:S(2)}, u32[]{:S(2)}) %collective-permute-start.2) | collective-permute-done | bytes 2097184 | tf_op jit(solution)/shard_map/ppermute | solution.py:14
  390.4 7.8 %shard_map.57 = f32[66,8,2,128,128]{4,3,2,1,0:T(8,128)} custom-call(s32[132]{0:T(256)S(1)} %reshape.169.slots_ref, f32[4,4,2,2,32,256]{5,4,3,2,1,0:T(8,128)S(1)} %copy-done, f32[4,4,2,2,32,256]{5,4,3,2,1,0:T(8,128)} %collective-permute-done.2.refs_1_, f32[8,128,1]{2,1,0:T(8,128)S(1)} %copy.77.refs_2_, ...), custom_call_target="tpu_custom_call", output_to_operand_aliasing={{}: (4, {})} | custom-call | flops 4831838208 | bytes 6291456 | tf_op jit(solution)/shard_map/pallas_call | solution.py:229
  (35 shorter events, 0.1 us)
Async XLA Ops:
  0.0 119.7 %copy-start.17 = (s32[64]{0:T(128)S(1)}, s32[64]{0:T(128)}, u32[]{:S(2)}) copy-start(s32[64]{0:T(128)} %param.5) | copy-start | bytes 772
  0.0 120.0 %copy-start.16 = (s32[66,2]{0,1:T(2,128)S(1)}, s32[66,2]{0,1:T(2,128)}, u32[]{:S(2)}) copy-start(s32[66,2]{0,1:T(2,128)} %param.4) | copy-start | bytes 1588
  115.6 75.9 %collective-permute-start.9 = (f32[4,4,2,2,32,256]{5,4,3,2,1,0:T(8,128)}, f32[4,4,2,2,32,256]{5,4,3,2,1,0:T(8,128)}, u32[]{:S(2)}, u32[]{:S(2)}) collective-permute-start(f32[4,4,2,2,32,256]{5,4,3,2,1,0:T(8,128)} %get-tuple-element.20.refs_1_), channel_id=1, source_target_pairs={{0,7},{1,0},{2,1},{3,2},{4,3},{5,4},{6,5},{7,6},{8,15},{9,8},{10,9... | collective-permute-start | bytes 6291464 | tf_op jit(solution)/shard_map/ppermute | solution.py:14
  119.4 72.2 %collective-permute-start.6 = (f32[4,4,2,2,32,256]{5,4,3,2,1,0:T(8,128)}, f32[4,4,2,2,32,256]{5,4,3,2,1,0:T(8,128)}, u32[]{:S(2)}, u32[]{:S(2)}) collective-permute-start(f32[4,4,2,2,32,256]{5,4,3,2,1,0:T(8,128)} %get-tuple-element.18.refs_1_), channel_id=1, source_target_pairs={{0,7},{1,0},{2,1},{3,2},{4,3},{5,4},{6,5},{7,6},{8,15},{9,8},{10,9... | collective-permute-start | bytes 6291464 | tf_op jit(solution)/shard_map/ppermute | solution.py:14
  119.4 97.7 %collective-permute-start.3 = (f32[4,4,2,2,32,256]{5,4,3,2,1,0:T(8,128)}, f32[4,4,2,2,32,256]{5,4,3,2,1,0:T(8,128)}, u32[]{:S(2)}, u32[]{:S(2)}) collective-permute-start(f32[4,4,2,2,32,256]{5,4,3,2,1,0:T(8,128)} %get-tuple-element.16.refs_1_), channel_id=1, source_target_pairs={{0,7},{1,0},{2,1},{3,2},{4,3},{5,4},{6,5},{7,6},{8,15},{9,8},{10,9... | collective-permute-start | bytes 6291464 | tf_op jit(solution)/shard_map/ppermute | solution.py:14
  119.5 97.7 %collective-permute-start = (f32[4,4,2,2,32,256]{5,4,3,2,1,0:T(8,128)}, f32[4,4,2,2,32,256]{5,4,3,2,1,0:T(8,128)}, u32[]{:S(2)}, u32[]{:S(2)}) collective-permute-start(f32[4,4,2,2,32,256]{5,4,3,2,1,0:T(8,128)} %get-tuple-element.14.refs_1_), channel_id=1, source_target_pairs={{0,7},{1,0},{2,1},{3,2},{4,3},{5,4},{6,5},{7,6},{8,15},{9,8},{10,9... | collective-permute-start | bytes 6291464 | tf_op jit(solution)/shard_map/ppermute | solution.py:14
  121.2 1.6 copy-start.5
  122.8 6.6 %copy-start.3 = (f32[4,4,2,2,32,256]{5,4,3,2,1,0:T(8,128)S(1)}, f32[4,4,2,2,32,256]{5,4,3,2,1,0:T(8,128)}, u32[]{:S(2)}) copy-start(f32[4,4,2,2,32,256]{5,4,3,2,1,0:T(8,128)} %get-tuple-element.17.refs_0_) | copy-start | bytes 6291460
  129.4 6.6 %copy-start.1 = (f32[4,4,2,2,32,256]{5,4,3,2,1,0:T(8,128)S(1)}, f32[4,4,2,2,32,256]{5,4,3,2,1,0:T(8,128)}, u32[]{:S(2)}) copy-start(f32[4,4,2,2,32,256]{5,4,3,2,1,0:T(8,128)} %get-tuple-element.15.refs_0_) | copy-start | bytes 6291460
  136.0 6.6 %copy-start = (f32[4,4,2,2,32,256]{5,4,3,2,1,0:T(8,128)S(1)}, f32[4,4,2,2,32,256]{5,4,3,2,1,0:T(8,128)}, u32[]{:S(2)}) copy-start(f32[4,4,2,2,32,256]{5,4,3,2,1,0:T(8,128)} %get-tuple-element.13.refs_0_) | copy-start | bytes 6291460
  142.6 6.6 %copy-start.12 = (f32[4,4,2,2,32,256]{5,4,3,2,1,0:T(8,128)S(1)}, f32[4,4,2,2,32,256]{5,4,3,2,1,0:T(8,128)}, u32[]{:S(2)}) copy-start(f32[4,4,2,2,32,256]{5,4,3,2,1,0:T(8,128)} %get-tuple-element.20.refs_1_) | copy-start | bytes 6291460
  149.3 10.2 %copy-start.11 = (f32[4,4,2,2,32,256]{5,4,3,2,1,0:T(8,128)S(1)}, f32[4,4,2,2,32,256]{5,4,3,2,1,0:T(8,128)}, u32[]{:S(2)}) copy-start(f32[4,4,2,2,32,256]{5,4,3,2,1,0:T(8,128)} %get-tuple-element.18.refs_1_) | copy-start | bytes 6291460
  159.4 10.2 %copy-start.10 = (f32[4,4,2,2,32,256]{5,4,3,2,1,0:T(8,128)S(1)}, f32[4,4,2,2,32,256]{5,4,3,2,1,0:T(8,128)}, u32[]{:S(2)}) copy-start(f32[4,4,2,2,32,256]{5,4,3,2,1,0:T(8,128)} %get-tuple-element.16.refs_1_) | copy-start | bytes 6291460
  169.6 10.2 %copy-start.9 = (f32[4,4,2,2,32,256]{5,4,3,2,1,0:T(8,128)S(1)}, f32[4,4,2,2,32,256]{5,4,3,2,1,0:T(8,128)}, u32[]{:S(2)}) copy-start(f32[4,4,2,2,32,256]{5,4,3,2,1,0:T(8,128)} %get-tuple-element.14.refs_1_) | copy-start | bytes 6291460
  179.8 10.2 %copy-start.15 = (f32[8,128,1]{1,0,2:T(8,128)S(1)}, f32[8,128,1]{1,0,2:T(8,128)}, u32[]{:S(2)}) copy-start(f32[8,128,1]{1,0,2:T(8,128)} %get-tuple-element.28) | copy-start | bytes 12292
  179.8 11.2 %copy-start.14 = (f32[8,128,1]{1,0,2:T(8,128)S(1)}, f32[8,128,1]{1,0,2:T(8,128)}, u32[]{:S(2)}) copy-start(f32[8,128,1]{1,0,2:T(8,128)} %get-tuple-element.27) | copy-start | bytes 12292
  179.8 11.4 %copy-start.13 = (f32[8,128,1]{1,0,2:T(8,128)S(1)}, f32[8,128,1]{1,0,2:T(8,128)}, u32[]{:S(2)}) copy-start(f32[8,128,1]{1,0,2:T(8,128)} %get-tuple-element.29) | copy-start | bytes 12292
  191.5 14.4 %copy-start.4 = (f32[4,4,2,2,32,256]{5,4,3,2,1,0:T(8,128)S(1)}, f32[4,4,2,2,32,256]{5,4,3,2,1,0:T(8,128)}, u32[]{:S(2)}) copy-start(f32[4,4,2,2,32,256]{5,4,3,2,1,0:T(8,128)} %get-tuple-element.17.refs_0_) | copy-start | bytes 6291460
  191.5 49.2 %collective-permute-start.10 = (f32[4,4,2,2,32,256]{5,4,3,2,1,0:T(8,128)}, f32[4,4,2,2,32,256]{5,4,3,2,1,0:T(8,128)}, u32[]{:S(2)}, u32[]{:S(2)}) collective-permute-start(f32[4,4,2,2,32,256]{5,4,3,2,1,0:T(8,128)} %collective-permute-done.9.refs_1_), channel_id=1, source_target_pairs={{0,7},{1,0},{2,1},{3,2},{4,3},{5,4},{6,5},{7,6},{8,15},{9,8},{10,9... | collective-permute-start | bytes 6291464 | tf_op jit(solution)/shard_map/ppermute | solution.py:14
  191.6 64.0 %collective-permute-start.7 = (f32[4,4,2,2,32,256]{5,4,3,2,1,0:T(8,128)}, f32[4,4,2,2,32,256]{5,4,3,2,1,0:T(8,128)}, u32[]{:S(2)}, u32[]{:S(2)}) collective-permute-start(f32[4,4,2,2,32,256]{5,4,3,2,1,0:T(8,128)} %collective-permute-done.6.refs_1_), channel_id=1, source_target_pairs={{0,7},{1,0},{2,1},{3,2},{4,3},{5,4},{6,5},{7,6},{8,15},{9,8},{10,9... | collective-permute-start | bytes 6291464 | tf_op jit(solution)/shard_map/ppermute | solution.py:14
  191.8 1.8 copy-start.6
  193.6 1.0 copy-start.7
  194.6 11.2 %copy-start.8 = (f32[8,128,1]{2,1,0:T(8,128)S(1)}, f32[8,128,1]{2,1,0:T(8,128)}, u32[]{:S(2)}) copy-start(f32[8,128,1]{2,1,0:T(8,128)} %copy.69.refs_2_) | copy-start | bytes 12292
  205.9 12.4 %copy-start.2 = (f32[4,4,2,2,32,256]{5,4,3,2,1,0:T(8,128)S(1)}, f32[4,4,2,2,32,256]{5,4,3,2,1,0:T(8,128)}, u32[]{:S(2)}) copy-start(f32[4,4,2,2,32,256]{5,4,3,2,1,0:T(8,128)} %get-tuple-element.15.refs_0_) | copy-start | bytes 6291460
  217.1 64.6 %collective-permute-start.4 = (f32[4,4,2,2,32,256]{5,4,3,2,1,0:T(8,128)}, f32[4,4,2,2,32,256]{5,4,3,2,1,0:T(8,128)}, u32[]{:S(2)}, u32[]{:S(2)}) collective-permute-start(f32[4,4,2,2,32,256]{5,4,3,2,1,0:T(8,128)} %collective-permute-done.3.refs_1_), channel_id=1, source_target_pairs={{0,7},{1,0},{2,1},{3,2},{4,3},{5,4},{6,5},{7,6},{8,15},{9,8},{10,9... | collective-permute-start | bytes 6291464 | tf_op jit(solution)/shard_map/ppermute | solution.py:14
  217.2 83.3 %collective-permute-start.1 = (f32[4,4,2,2,32,256]{5,4,3,2,1,0:T(8,128)}, f32[4,4,2,2,32,256]{5,4,3,2,1,0:T(8,128)}, u32[]{:S(2)}, u32[]{:S(2)}) collective-permute-start(f32[4,4,2,2,32,256]{5,4,3,2,1,0:T(8,128)} %collective-permute-done.refs_1_), channel_id=1, source_target_pairs={{0,7},{1,0},{2,1},{3,2},{4,3},{5,4},{6,5},{7,6},{8,15},{9,8},{10,9... | collective-permute-start | bytes 6291464 | tf_op jit(solution)/shard_map/ppermute | solution.py:14
  240.7 82.3 %collective-permute-start.11 = (f32[4,4,2,2,32,256]{5,4,3,2,1,0:T(8,128)}, f32[4,4,2,2,32,256]{5,4,3,2,1,0:T(8,128)}, u32[]{:S(2)}, u32[]{:S(2)}) collective-permute-start(f32[4,4,2,2,32,256]{5,4,3,2,1,0:T(8,128)} %collective-permute-done.10.refs_1_), channel_id=1, source_target_pairs={{0,7},{1,0},{2,1},{3,2},{4,3},{5,4},{6,5},{7,6},{8,15},{9,8},{10,9... | collective-permute-start | bytes 6291464 | tf_op jit(solution)/shard_map/ppermute | solution.py:14
  255.6 89.9 %collective-permute-start.8 = (f32[4,4,2,2,32,256]{5,4,3,2,1,0:T(8,128)}, f32[4,4,2,2,32,256]{5,4,3,2,1,0:T(8,128)}, u32[]{:S(2)}, u32[]{:S(2)}) collective-permute-start(f32[4,4,2,2,32,256]{5,4,3,2,1,0:T(8,128)} %collective-permute-done.7.refs_1_), channel_id=1, source_target_pairs={{0,7},{1,0},{2,1},{3,2},{4,3},{5,4},{6,5},{7,6},{8,15},{9,8},{10,9... | collective-permute-start | bytes 6291464 | tf_op jit(solution)/shard_map/ppermute | solution.py:14
  281.7 86.2 %collective-permute-start.5 = (f32[4,4,2,2,32,256]{5,4,3,2,1,0:T(8,128)}, f32[4,4,2,2,32,256]{5,4,3,2,1,0:T(8,128)}, u32[]{:S(2)}, u32[]{:S(2)}) collective-permute-start(f32[4,4,2,2,32,256]{5,4,3,2,1,0:T(8,128)} %collective-permute-done.4.refs_1_), channel_id=1, source_target_pairs={{0,7},{1,0},{2,1},{3,2},{4,3},{5,4},{6,5},{7,6},{8,15},{9,8},{10,9... | collective-permute-start | bytes 6291464 | tf_op jit(solution)/shard_map/ppermute | solution.py:14
  300.5 89.9 %collective-permute-start.2 = (f32[4,4,2,2,32,256]{5,4,3,2,1,0:T(8,128)}, f32[4,4,2,2,32,256]{5,4,3,2,1,0:T(8,128)}, u32[]{:S(2)}, u32[]{:S(2)}) collective-permute-start(f32[4,4,2,2,32,256]{5,4,3,2,1,0:T(8,128)} %collective-permute-done.1.refs_1_), channel_id=1, source_target_pairs={{0,7},{1,0},{2,1},{3,2},{4,3},{5,4},{6,5},{7,6},{8,15},{9,8},{10,9... | collective-permute-start | bytes 6291464 | tf_op jit(solution)/shard_map/ppermute | solution.py:14
